TPU v7x, 32 devices: a whole 2x2x4 slice. The times are simulated.
32 devices in a mesh: groups: 2 (over x), leaf: 16 (over z, y, core).
Axes of the slice: x: 2, y: 2, z: 4, core: 2. Of those that a mesh axis runs over, the one named last changes fastest.
Arguments:
- points: float32 [3, 131072], P(None, ('groups', 'leaf')), parts along dimension 1, may hold values from 0 to 1.6, as said below
- input_vectors: float32 [64, 131072], P(None, ('groups', 'leaf')), parts along dimension 1, may hold values from -6 to 6
- leaf_basis: float32 [512, 64, 256], P(('groups', 'leaf')), parts along dimension 0, may hold values from -0.375 to 0.375
- transfer_one: float32 [256, 64, 128], P(('groups', 'leaf')), parts along dimension 0, may hold values from -0.5 to 0.5
- transfer_two: float32 [128, 64, 128], P(('groups', 'leaf')), parts along dimension 0, may hold values from -0.5 to 0.5
- coupling_zero: float32 [512, 64, 512], P(('groups', 'leaf')), parts along dimension 0, may hold values from -0.25 to 0.25
- coupling_one: float32 [256, 64, 512], P(('groups', 'leaf')), parts along dimension 0, may hold values from -0.25 to 0.25
- coupling_two: float32 [128, 64, 512], P(('groups', 'leaf')), parts along dimension 0, may hold values from -0.25 to 0.25
- neighbour_leaves: int32 [512, 16], P(('groups', 'leaf')), parts along dimension 0, may hold values from 0 to 255, as said below
- far_zero: int32 [512, 8], P(('groups', 'leaf')), parts along dimension 0, may hold values from 0 to 255, as said below
- far_one: int32 [256, 8], P(('groups', 'leaf')), parts along dimension 0, may hold values from 0 to 127, as said below
- far_two: int32 [128, 8], P(('groups', 'leaf')), parts along dimension 0, may hold values from 0 to 63, as said below
Outputs:
- kernel_product: float32 [64, 131072], P(None, ('groups', 'leaf')), parts along dimension 1
There are 2 independent parts, one for each index of `groups`. A program takes and returns all parts, laid end to end along the dimension named above; each array names one. Nothing has to cross between parts.
Inputs may be any that keep to these rules, and one draw needn't show every extreme that they name: Each leaf's points lie in a box of side 0.1 of its own; the leaves of one device block of 16 leaves fill one layer of boxes along the third coordinate, in block order. `neighbour_leaves`: entry 0 of a leaf's row is the leaf itself; the others are leaves of the same device block of 16 leaves or of the block just before or after it, and may repeat. `far_zero`: Level-0 nodes are held in blocks of 16; the rows of one block name at most 16 entries, counted with repetition, of any single block, and every block's rows reach that bound for some block. No leaf names itself. `far_one`: Level-1 nodes are held in blocks of 8; the rows of one block name at most 8 entries of any single block, reached by every block's rows. No node names itself. `far_two`: Level-2 nodes are held in blocks of 4; the rows of one block name at most 4 entries of any single block, reached by every block's rows. No node names itself.
All inputs are finite; a program needn't handle non-finite values.
Results may differ from a plain program's by a relative error of at most 0.0003.
Values sent between devices are 32-bit elements; how exact they have to be, the bound alone decides.
No kernel may reach another device: no remote copies, remote signals or barrier semaphores. Data moves between devices by JAX's collectives and lax.ppermute only.
A program may use at most 128 MiB of HBM per device.

v0:
```python
import math

import jax
import jax.numpy as jnp
from jax import lax
from jax.sharding import PartitionSpec as P

highest = lax.Precision.HIGHEST
inverse_scale = math.sqrt(3.0) / 0.05


def padded(value, sides, width):
    for axis, dim in sides:
        size, length = (lax.axis_size(axis), value.shape[dim])
        up = [(i, (i + 1) % size) for i in range(size - 1)]
        down = [(j, i) for i, j in up]
        last = lax.slice_in_dim(value, length - width, length, axis=dim)
        first = lax.slice_in_dim(value, 0, width, axis=dim)
        before = lax.ppermute(last, axis, up)
        after = lax.ppermute(first, axis, down)
        value = jnp.concatenate([before, value, after], axis=dim)
    return value


def matern(squared):
    distance = jnp.sqrt(jnp.maximum(squared, 0.0)) * inverse_scale
    return (1.0 + distance) * jnp.exp(-distance)


def block_contributions(accumulator, evaluation_points, partner_indices):
    source_points = accumulator[:, partner_indices]
    squared = (source_points[0][:, :, :, None] - evaluation_points[0][:, None, None, :]) ** 2
    squared = (
        squared + (source_points[1][:, :, :, None] - evaluation_points[1][:, None, None, :]) ** 2
    )
    squared = (
        squared + (source_points[2][:, :, :, None] - evaluation_points[2][:, None, None, :]) ** 2
    )
    kernel = matern(squared)
    return jnp.einsum("nbks,bkst->nbt", source_points[3:], kernel, precision=highest)


def nearby_interaction(accumulator, points, partner_indices):
    leaf_clusters = partner_indices.shape[0]
    points_per_leaf = points.shape[1] // leaf_clusters
    blocks = leaf_clusters // 2
    targets = jnp.transpose(points.reshape(3, blocks, 2, points_per_leaf), (1, 0, 2, 3))
    partners = partner_indices.reshape(blocks, 2, -1)

    def one_block(element):
        return block_contributions(accumulator, element[0], element[1])

    output_blocks = lax.map(one_block, (targets, partners))
    return jnp.transpose(output_blocks, (1, 0, 2, 3)).reshape(accumulator.shape[0] - 3, -1)


def fetch_far(coeffs, partners):
    node_count = coeffs.shape[0]
    flattened = coeffs.reshape(node_count, -1)
    wanted_ids = partners.reshape(-1)
    everything = lax.all_gather(flattened, "leaf", axis=0, tiled=True)
    picked = jnp.take(everything, wanted_ids, axis=0)
    return picked.reshape(node_count, -1, coeffs.shape[2])


def on_device(
    points,
    input_vectors,
    leaf_basis,
    transfer_one,
    transfer_two,
    coupling_zero,
    coupling_one,
    coupling_two,
    neighbour_leaves,
    far_zero,
    far_one,
    far_two,
):
    leaf_clusters = leaf_basis.shape[0]
    rank_size = leaf_basis.shape[1]
    rhs_count = input_vectors.shape[0]
    points_per_leaf = points.shape[1] // leaf_clusters
    accumulator = jnp.concatenate([points, input_vectors], axis=0)
    broadened = padded(accumulator, (("leaf", 1),), points.shape[1])
    broadened = broadened.reshape(accumulator.shape[0], 3 * leaf_clusters, points_per_leaf)
    first_leaf = (lax.axis_index("leaf") - 1) * leaf_clusters
    columns = input_vectors.reshape(rhs_count, leaf_clusters, points_per_leaf)
    coeff_zero = jnp.einsum("lrs,nls->lrn", leaf_basis, columns, precision=highest)
    coeff_one = jnp.einsum(
        "prc,pcn->prn",
        transfer_one,
        coeff_zero.reshape(leaf_clusters // 2, 2 * rank_size, rhs_count),
        precision=highest,
    )
    coeff_two = jnp.einsum(
        "prc,pcn->prn",
        transfer_two,
        coeff_one.reshape(leaf_clusters // 4, 2 * rank_size, rhs_count),
        precision=highest,
    )
    fields = []
    for coupling, coeffs, partners in (
        (coupling_zero, coeff_zero, far_zero),
        (coupling_one, coeff_one, far_one),
        (coupling_two, coeff_two, far_two),
    ):
        stacked = fetch_far(coeffs, partners)
        fields.append(jnp.einsum("trj,tjn->trn", coupling, stacked, precision=highest))
    nearby_portion = nearby_interaction(broadened, points, neighbour_leaves - first_leaf)
    down_one = fields[1] + jnp.einsum(
        "prc,prn->pcn", transfer_two, fields[2], precision=highest
    ).reshape(leaf_clusters // 2, rank_size, rhs_count)
    down_zero = fields[0] + jnp.einsum(
        "prc,prn->pcn", transfer_one, down_one, precision=highest
    ).reshape(leaf_clusters, rank_size, rhs_count)
    far_part = jnp.einsum("lrn,lrs->nls", down_zero, leaf_basis, precision=highest).reshape(
        rhs_count, -1
    )
    return nearby_portion + far_part


def solution(mesh):
    return jax.shard_map(
        on_device,
        mesh=mesh,
        in_specs=(
            P(None, ("groups", "leaf")),
            P(None, ("groups", "leaf")),
            P(("groups", "leaf"), None, None),
            P(("groups", "leaf"), None, None),
            P(("groups", "leaf"), None, None),
            P(("groups", "leaf"), None, None),
            P(("groups", "leaf"), None, None),
            P(("groups", "leaf"), None, None),
            P(("groups", "leaf"), None),
            P(("groups", "leaf"), None),
            P(("groups", "leaf"), None),
            P(("groups", "leaf"), None),
        ),
        out_specs=P(None, ("groups", "leaf")),
        check_vma=False,
    )
```

profile of v0, /device:TPU:9, one launch (start us, length us, event | category | flops | bytes accessed | tf_op | source)
XLA Modules:
  0.0 270.5 jit_solution(16427135722719938643)
XLA Ops:
  23.9 3.7 %collective-permute-start = (f32[67,4096]{1,0:T(8,128)}, f32[67,4096]{1,0:T(8,128)}, u32[]{:S(2)}, u32[]{:S(2)}) collective-permute-start(f32[67,4096]{1,0:T(8,128)} %pad_maximum_fusion.1), channel_id=1, source_target_pairs={{0,1},{1,2},{2,3},{3,4},{4,5},{5,6},{6,7},{7,8},{8,9},{9,10},{10,1... | collective-permute-start | bytes 3293192 | tf_op jit(solution)/shard_map/ppermute | solution.py:19
  32.8 24.3 %collective-permute-done = f32[67,4096]{1,0:T(8,128)} collective-permute-done((f32[67,4096]{1,0:T(8,128)}, f32[67,4096]{1,0:T(8,128)}, u32[]{:S(2)}, u32[]{:S(2)}) %collective-permute-start) | collective-permute-done | bytes 1097760 | tf_op jit(solution)/shard_map/ppermute | solution.py:19
  62.2 3.7 %copy.53 = f32[67,48,256]{2,0,1:T(8,128)} copy(f32[67,48,256]{2,1,0:T(8,128)S(1)} %slice.39) | data formatting | bytes 6586368 | tf_op jit(solution)/shard_map/while | solution.py:53
  65.9 151.1 %while.10 = (s32[]{:T(128)}, f32[8,64,2,256]{3,1,2,0:T(8,128)}, s32[8,2,16]{2,1,0:T(2,128)S(1)}, f32[67,48,256]{2,0,1:T(8,128)}, f32[8,3,2,256]{3,2,0,1:T(2,128)S(1)}, /*index=5*/s32[]{:T(128)}) while((s32[]{:T(128)}, f32[8,64,2,256]{3,1,2,0:T(8,128)}, s32[8,2,16]{2,1,0:T(2,128)S(1)}, f32[67,48,256]{2,0,1:T(8,128)}, ...), condition=%wide.region_1.2_spmd, body=%wide.region_0.1_spmd.sunk | while | flops 1637876864 | bytes 7146829 | solution.py:53
  66.0 4.2 %gather_fusion = f32[32,67,256]{2,1,0:T(8,128)} fusion(f32[67,48,256]{2,0,1:T(8,128)} %get-tuple-element.128, s32[1024]{0:T(1024)S(1)} %pad_clamp_fusion.5), kind=kCustom, calls=%fused_computation.clone.1 | custom fusion | bytes 4391040 | tf_op jit(solution)/shard_map/while/body/eval_jaxpr/gather | solution.py:31
  71.6 13.2 %fusion.94 = f32[8,64,2,256]{3,1,2,0:T(8,128)} fusion(f32[8,64,2,256]{3,1,2,0:T(8,128)} %get-tuple-element.120, s32[]{:T(128)} %get-tuple-element.119, f32[67,2,16,256]{3,0,2,1:T(8,128)} %bitcast.102, f32[2,256]{1,0:T(2,128)S(1)} %get-tuple-element.105, f32[2,16,256]{2,1,0:T(8,128)S(1)} %get-tuple-element.108, f32[2,256]{1,0:T(2,128)S(1)} %get-tuple-element.109, ...), kind=kOutput, calls=%fused_computation.31.clone.1 | convolution fusion | flops 1637875712 | bytes 2333184 | tf_op jit(solution)/shard_map/while/body/eval_jaxpr/nbks,bkst->nbt/dot_general | solution.py:40
  84.9 4.2 %gather_fusion = f32[32,67,256]{2,1,0:T(8,128)} fusion(f32[67,48,256]{2,0,1:T(8,128)} %get-tuple-element.128, s32[1024]{0:T(1024)S(1)} %pad_clamp_fusion.5), kind=kCustom, calls=%fused_computation.clone.1 | custom fusion | bytes 4391040 | tf_op jit(solution)/shard_map/while/body/eval_jaxpr/gather | solution.py:31
  90.5 13.2 %fusion.94 = f32[8,64,2,256]{3,1,2,0:T(8,128)} fusion(f32[8,64,2,256]{3,1,2,0:T(8,128)} %get-tuple-element.120, s32[]{:T(128)} %get-tuple-element.119, f32[67,2,16,256]{3,0,2,1:T(8,128)} %bitcast.102, f32[2,256]{1,0:T(2,128)S(1)} %get-tuple-element.105, f32[2,16,256]{2,1,0:T(8,128)S(1)} %get-tuple-element.108, f32[2,256]{1,0:T(2,128)S(1)} %get-tuple-element.109, ...), kind=kOutput, calls=%fused_computation.31.clone.1 | convolution fusion | flops 1637875712 | bytes 2333184 | tf_op jit(solution)/shard_map/while/body/eval_jaxpr/nbks,bkst->nbt/dot_general | solution.py:40
  103.8 4.2 %gather_fusion = f32[32,67,256]{2,1,0:T(8,128)} fusion(f32[67,48,256]{2,0,1:T(8,128)} %get-tuple-element.128, s32[1024]{0:T(1024)S(1)} %pad_clamp_fusion.5), kind=kCustom, calls=%fused_computation.clone.1 | custom fusion | bytes 4391040 | tf_op jit(solution)/shard_map/while/body/eval_jaxpr/gather | solution.py:31
  109.4 13.2 %fusion.94 = f32[8,64,2,256]{3,1,2,0:T(8,128)} fusion(f32[8,64,2,256]{3,1,2,0:T(8,128)} %get-tuple-element.120, s32[]{:T(128)} %get-tuple-element.119, f32[67,2,16,256]{3,0,2,1:T(8,128)} %bitcast.102, f32[2,256]{1,0:T(2,128)S(1)} %get-tuple-element.105, f32[2,16,256]{2,1,0:T(8,128)S(1)} %get-tuple-element.108, f32[2,256]{1,0:T(2,128)S(1)} %get-tuple-element.109, ...), kind=kOutput, calls=%fused_computation.31.clone.1 | convolution fusion | flops 1637875712 | bytes 2333184 | tf_op jit(solution)/shard_map/while/body/eval_jaxpr/nbks,bkst->nbt/dot_general | solution.py:40
  122.7 4.2 %gather_fusion = f32[32,67,256]{2,1,0:T(8,128)} fusion(f32[67,48,256]{2,0,1:T(8,128)} %get-tuple-element.128, s32[1024]{0:T(1024)S(1)} %pad_clamp_fusion.5), kind=kCustom, calls=%fused_computation.clone.1 | custom fusion | bytes 4391040 | tf_op jit(solution)/shard_map/while/body/eval_jaxpr/gather | solution.py:31
  128.3 13.2 %fusion.94 = f32[8,64,2,256]{3,1,2,0:T(8,128)} fusion(f32[8,64,2,256]{3,1,2,0:T(8,128)} %get-tuple-element.120, s32[]{:T(128)} %get-tuple-element.119, f32[67,2,16,256]{3,0,2,1:T(8,128)} %bitcast.102, f32[2,256]{1,0:T(2,128)S(1)} %get-tuple-element.105, f32[2,16,256]{2,1,0:T(8,128)S(1)} %get-tuple-element.108, f32[2,256]{1,0:T(2,128)S(1)} %get-tuple-element.109, ...), kind=kOutput, calls=%fused_computation.31.clone.1 | convolution fusion | flops 1637875712 | bytes 2333184 | tf_op jit(solution)/shard_map/while/body/eval_jaxpr/nbks,bkst->nbt/dot_general | solution.py:40
  141.6 4.2 %gather_fusion = f32[32,67,256]{2,1,0:T(8,128)} fusion(f32[67,48,256]{2,0,1:T(8,128)} %get-tuple-element.128, s32[1024]{0:T(1024)S(1)} %pad_clamp_fusion.5), kind=kCustom, calls=%fused_computation.clone.1 | custom fusion | bytes 4391040 | tf_op jit(solution)/shard_map/while/body/eval_jaxpr/gather | solution.py:31
  147.2 13.2 %fusion.94 = f32[8,64,2,256]{3,1,2,0:T(8,128)} fusion(f32[8,64,2,256]{3,1,2,0:T(8,128)} %get-tuple-element.120, s32[]{:T(128)} %get-tuple-element.119, f32[67,2,16,256]{3,0,2,1:T(8,128)} %bitcast.102, f32[2,256]{1,0:T(2,128)S(1)} %get-tuple-element.105, f32[2,16,256]{2,1,0:T(8,128)S(1)} %get-tuple-element.108, f32[2,256]{1,0:T(2,128)S(1)} %get-tuple-element.109, ...), kind=kOutput, calls=%fused_computation.31.clone.1 | convolution fusion | flops 1637875712 | bytes 2333184 | tf_op jit(solution)/shard_map/while/body/eval_jaxpr/nbks,bkst->nbt/dot_general | solution.py:40
  160.5 4.2 %gather_fusion = f32[32,67,256]{2,1,0:T(8,128)} fusion(f32[67,48,256]{2,0,1:T(8,128)} %get-tuple-element.128, s32[1024]{0:T(1024)S(1)} %pad_clamp_fusion.5), kind=kCustom, calls=%fused_computation.clone.1 | custom fusion | bytes 4391040 | tf_op jit(solution)/shard_map/while/body/eval_jaxpr/gather | solution.py:31
  166.1 13.2 %fusion.94 = f32[8,64,2,256]{3,1,2,0:T(8,128)} fusion(f32[8,64,2,256]{3,1,2,0:T(8,128)} %get-tuple-element.120, s32[]{:T(128)} %get-tuple-element.119, f32[67,2,16,256]{3,0,2,1:T(8,128)} %bitcast.102, f32[2,256]{1,0:T(2,128)S(1)} %get-tuple-element.105, f32[2,16,256]{2,1,0:T(8,128)S(1)} %get-tuple-element.108, f32[2,256]{1,0:T(2,128)S(1)} %get-tuple-element.109, ...), kind=kOutput, calls=%fused_computation.31.clone.1 | convolution fusion | flops 1637875712 | bytes 2333184 | tf_op jit(solution)/shard_map/while/body/eval_jaxpr/nbks,bkst->nbt/dot_general | solution.py:40
  179.4 4.2 %gather_fusion = f32[32,67,256]{2,1,0:T(8,128)} fusion(f32[67,48,256]{2,0,1:T(8,128)} %get-tuple-element.128, s32[1024]{0:T(1024)S(1)} %pad_clamp_fusion.5), kind=kCustom, calls=%fused_computation.clone.1 | custom fusion | bytes 4391040 | tf_op jit(solution)/shard_map/while/body/eval_jaxpr/gather | solution.py:31
  185.0 13.2 %fusion.94 = f32[8,64,2,256]{3,1,2,0:T(8,128)} fusion(f32[8,64,2,256]{3,1,2,0:T(8,128)} %get-tuple-element.120, s32[]{:T(128)} %get-tuple-element.119, f32[67,2,16,256]{3,0,2,1:T(8,128)} %bitcast.102, f32[2,256]{1,0:T(2,128)S(1)} %get-tuple-element.105, f32[2,16,256]{2,1,0:T(8,128)S(1)} %get-tuple-element.108, f32[2,256]{1,0:T(2,128)S(1)} %get-tuple-element.109, ...), kind=kOutput, calls=%fused_computation.31.clone.1 | convolution fusion | flops 1637875712 | bytes 2333184 | tf_op jit(solution)/shard_map/while/body/eval_jaxpr/nbks,bkst->nbt/dot_general | solution.py:40
  198.2 4.2 %gather_fusion = f32[32,67,256]{2,1,0:T(8,128)} fusion(f32[67,48,256]{2,0,1:T(8,128)} %get-tuple-element.128, s32[1024]{0:T(1024)S(1)} %pad_clamp_fusion.5), kind=kCustom, calls=%fused_computation.clone.1 | custom fusion | bytes 4391040 | tf_op jit(solution)/shard_map/while/body/eval_jaxpr/gather | solution.py:31
  203.9 13.2 %fusion.94 = f32[8,64,2,256]{3,1,2,0:T(8,128)} fusion(f32[8,64,2,256]{3,1,2,0:T(8,128)} %get-tuple-element.120, s32[]{:T(128)} %get-tuple-element.119, f32[67,2,16,256]{3,0,2,1:T(8,128)} %bitcast.102, f32[2,256]{1,0:T(2,128)S(1)} %get-tuple-element.105, f32[2,16,256]{2,1,0:T(8,128)S(1)} %get-tuple-element.108, f32[2,256]{1,0:T(2,128)S(1)} %get-tuple-element.109, ...), kind=kOutput, calls=%fused_computation.31.clone.1 | convolution fusion | flops 1637875712 | bytes 2333184 | tf_op jit(solution)/shard_map/while/body/eval_jaxpr/nbks,bkst->nbt/dot_general | solution.py:40
  234.4 6.0 %fusion.54 = f32[8,64,64]{1,2,0:T(8,128)S(1)} fusion(f32[8,64,512]{2,1,0:T(8,128)} %param.20, f32[8,512,64]{2,1,0:T(8,128)} %gather.24, pred[8,512]{1,0:T(8,128)(4,1)S(1)} %broadcast_in_dim.56, f32[8,64,64]{1,0,2:T(8,128)S(1)} %reshape.215), kind=kOutput, calls=%fused_computation.58 | convolution fusion | flops 201621504 | bytes 2363392 | tf_op jit(solution)/shard_map/trj,tjn->trn/dot_general | solution.py:109
  241.1 5.9 %gather_fusion.1 = f32[128,4096]{1,0:T(8,128)} fusion(f32[256,4096]{1,0:T(8,128)} %all-gather.5.cloned.1.call-done, s32[1024]{0:T(1024)S(1)} %pad_clamp_fusion.3), kind=kCustom, calls=%fused_computation.1 | custom fusion | bytes 4194816 | tf_op jit(solution)/shard_map/jit(_take)/gather | solution.py:62
  247.1 4.6 %gather.22 = f32[16,512,64]{2,1,0:T(8,128)} reshape(f32[128,4096]{1,0:T(8,128)} %gather_fusion.1) | data formatting | bytes 4194304 | tf_op jit(solution)/shard_map/jit(_take)/gather | solution.py:62
  251.6 10.0 %fusion.48 = f32[16,64,64]{1,2,0:T(8,128)S(1)} fusion(f32[16,64,512]{2,1,0:T(8,128)S(1)} %copy-done, f32[16,512,64]{2,1,0:T(8,128)} %gather.22, pred[16,512]{1,0:T(8,128)(4,1)S(1)} %broadcast_in_dim.52, f32[16,64,64]{1,0,2:T(8,128)S(1)} %reshape.216), kind=kOutput, calls=%fused_computation.53 | convolution fusion | flops 403243008 | bytes 4726784 | tf_op jit(solution)/shard_map/trj,tjn->trn/dot_general | solution.py:109
  (153 shorter events, 59.8 us)
Async XLA Ops:
  6.5 245.1 %copy-start = (f32[16,64,512]{2,1,0:T(8,128)S(1)}, f32[16,64,512]{2,1,0:T(8,128)}, u32[]{:S(2)}) copy-start(f32[16,64,512]{2,1,0:T(8,128)} %param.19) | copy-start | bytes 6291460
  6.5 16.1 %copy-start.1 = (f32[64,4096]{1,0:T(8,128)S(1)}, f32[64,4096]{1,0:T(8,128)}, u32[]{:S(2)}) copy-start(f32[64,4096]{1,0:T(8,128)} %param.15) | copy-start | bytes 3145732
  6.5 16.2 %copy-start.6 = (f32[3,4096]{1,0:T(4,128)S(1)}, f32[3,4096]{1,0:T(4,128)}, u32[]{:S(2)}) copy-start(f32[3,4096]{1,0:T(4,128)} %param.14) | copy-start | bytes 147460
  6.5 214.3 %all-gather.9.cloned.1.call-start = ((), (), s32[]{:S(2)}) async-start(), calls=%async_computation.2 | async-start | bytes 1114112 | tf_op jit(solution)/shard_map/all_gather | solution.py:61
  9.3 0.8 copy-start.2
  10.1 21.5 %copy-start.10 = (s32[4,8]{1,0:T(4,128)S(1)}, s32[4,8]{1,0:T(4,128)}, u32[]{:S(2)}) copy-start(s32[4,8]{1,0:T(4,128)} %param.25) | copy-start | bytes 388
  10.1 21.6 %copy-start.9 = (s32[8,8]{1,0:T(8,128)S(1)}, s32[8,8]{1,0:T(8,128)}, u32[]{:S(2)}) copy-start(s32[8,8]{1,0:T(8,128)} %param.24) | copy-start | bytes 772
  10.1 21.7 %copy-start.8 = (s32[16,8]{0,1:T(8,128)S(1)}, s32[16,8]{0,1:T(8,128)}, u32[]{:S(2)}) copy-start(s32[16,8]{0,1:T(8,128)} %param.23) | copy-start | bytes 1540
  10.1 22.7 %copy-start.11 = (s32[16,16]{1,0:T(8,128)S(1)}, s32[16,16]{1,0:T(8,128)}, u32[]{:S(2)}) copy-start(s32[16,16]{1,0:T(8,128)} %param.22) | copy-start | bytes 3076
  20.0 209.2 %all-gather.7.cloned.1.call-start = ((), (), s32[]{:S(2)}) async-start(), calls=%async_computation.1 | async-start | bytes 2228224 | tf_op jit(solution)/shard_map/all_gather | solution.py:61
  22.6 218.5 %all-gather.5.cloned.1.call-start = ((), (), s32[]{:S(2)}) async-start(), calls=%async_computation | async-start | bytes 4456448 | tf_op jit(solution)/shard_map/all_gather | solution.py:61
  23.9 33.3 %collective-permute-start = (f32[67,4096]{1,0:T(8,128)}, f32[67,4096]{1,0:T(8,128)}, u32[]{:S(2)}, u32[]{:S(2)}) collective-permute-start(f32[67,4096]{1,0:T(8,128)} %pad_maximum_fusion.1), channel_id=1, source_target_pairs={{0,1},{1,2},{2,3},{3,4},{4,5},{5,6},{6,7},{7,8},{8,9},{9,10},{10,1... | collective-permute-start | bytes 3293192 | tf_op jit(solution)/shard_map/ppermute | solution.py:19
  27.6 31.4 %collective-permute-start.1 = (f32[67,4096]{1,0:T(8,128)}, f32[67,4096]{1,0:T(8,128)}, u32[]{:S(2)}, u32[]{:S(2)}) collective-permute-start(f32[67,4096]{1,0:T(8,128)} %pad_maximum_fusion.1), channel_id=1, source_target_pairs={{1,0},{2,1},{3,2},{4,3},{5,4},{6,5},{7,6},{8,7},{9,8},{10,9},{11,1... | collective-permute-start | bytes 3293192 | tf_op jit(solution)/shard_map/ppermute | solution.py:20
  222.5 6.2 %copy-start.7 = (f32[4,64,128]{2,1,0:T(8,128)S(1)}, f32[4,64,128]{2,1,0:T(8,128)}, u32[]{:S(2)}) copy-start(f32[4,64,128]{2,1,0:T(8,128)} %param.18) | copy-start | bytes 393220
  234.4 6.0 %copy-start.5 = (f32[8,64,128]{2,1,0:T(8,128)S(1)}, f32[8,64,128]{2,1,0:T(8,128)}, u32[]{:S(2)}) copy-start(f32[8,64,128]{2,1,0:T(8,128)} %param.17) | copy-start | bytes 786436
  251.6 10.0 %copy-start.4 = (f32[16,64,256]{2,1,0:T(8,128)S(1)}, f32[16,64,256]{2,1,0:T(8,128)}, u32[]{:S(2)}) copy-start(f32[16,64,256]{2,1,0:T(8,128)} %param.16) | copy-start | bytes 3145732
  261.6 1.2 copy-start.3
Sparse Core Ops, SparseCore 0:
  20.1 40.4 all-gather.8
  62.8 40.3 all-gather.6
  105.4 50.2 all-gather.4
where the time goes:
time: 272 us; the launch traced here: 270 us
  matrix products  133 us (49%)
  local copies, waits for them, and re-layouts  87.3 us (32%)
  waiting for transfers between devices  26.3 us (10%)
  between operations  13.5 us (5%)
  starting transfers between devices  5.88 us (2%)
  other arithmetic  4.32 us (2%)
    dot_general x8, matrix products, block_contributions(): jnp.einsum('nbks,bkst->nbt', source_points[3:], kernel, precision=highest)  105 us
    gather x8, local copies, waits for them, and re-layouts, block_contributions(): source_points = accumulator[:, partner_indices]  33.4 us
    ppermute x1, waiting for transfers between devices, padded(): before = lax.ppermute(last, axis, up)  24.3 us
    dot_general x3, matrix products, on_device(): jnp.einsum('trj,tjn->trn', coupling, stacked, precision=highest)  19.2 us
    gather x6, local copies, waits for them, and re-layouts, fetch_far(): picked = jnp.take(everything, wanted_ids, axis=0)  18.6 us
    slice x8, local copies, waits for them, and re-layouts, block_contributions(): source_points[0][:, :, :, None] - evaluation_points[0][:, None, None, :]  11.1 us
  transfers between devices with their start and end apart: 5, of which 2 were waited for; matrix products, arithmetic and copies ran while one was open for 70% of the time, Pallas kernels for 0%

commit v1 on v0

v1 whole, which is shorter than its diff:
```python
import functools
import math

import jax
import jax.numpy as jnp
from jax import lax
from jax.experimental import pallas as pl
from jax.experimental.pallas import tpu as pltpu
from jax.sharding import PartitionSpec as P

LOG2E = math.log2(math.e)
LN2 = math.log(2.0)
SCALE = math.sqrt(3.0) / 0.05 * LOG2E
TINY = 1e-10
NN = (((1,), (0,)), ((), ()))
NT = (((1,), (1,)), ((), ()))
VMEM_LIMIT = 56 * 1024 * 1024


def halves(value):
    high = value.astype(jnp.bfloat16)
    low = (value - high.astype(jnp.float32)).astype(jnp.bfloat16)
    return high, low


def product(left, right, dims):
    left_high, left_low = halves(left)
    right_high, right_low = halves(right)
    dot = functools.partial(lax.dot_general, preferred_element_type=jnp.float32)
    return (
        dot(left_high, right_high, dims)
        + dot(left_high, right_low, dims)
        + dot(left_low, right_high, dims)
    )


def up_kernel(vectors, basis, first, second, out):
    leaves, _, size = basis.shape
    rank = basis.shape[1]
    pairs = []
    for pair in range(leaves // 2):
        both = []
        for leaf in (2 * pair, 2 * pair + 1):
            columns = vectors[:, leaf * size : (leaf + 1) * size]
            both.append(product(columns, basis[leaf], NT))
        pairs.append(jnp.concatenate(both, axis=1))
        out[pair] = pairs[pair]
    base = len(pairs)
    for transfer in (first, second):
        nodes = [product(pairs[i], transfer[i], NT) for i in range(len(pairs))]
        pairs = [
            jnp.concatenate(nodes[2 * i : 2 * i + 2], axis=1) for i in range(len(nodes) // 2)
        ]
        for i, pair in enumerate(pairs):
            out[base + i] = pair
        base += len(pairs)


def thirds(value):
    high = value.astype(jnp.bfloat16).astype(jnp.float32)
    rest = value - high
    middle = rest.astype(jnp.bfloat16).astype(jnp.float32)
    low = (rest - middle).astype(jnp.bfloat16).astype(jnp.float32)
    return high, middle, low


def features(points, centre, source):
    scaled = (points - centre) * SCALE
    high, middle, low = thirds(scaled)
    square = jnp.sum(scaled * scaled, axis=0, keepdims=True)
    parts = jnp.concatenate(thirds(square), axis=0)
    ones = jnp.ones_like(parts)
    pad = jnp.zeros((8, points.shape[1]), jnp.float32)
    if source:
        rows = [high, high, middle, middle, high, low, parts, ones, pad]
    else:
        rows = [-2.0 * v for v in (high, middle, high, middle, low, high)]
        rows += [ones, parts, pad]
    return jnp.concatenate(rows, axis=0)


def near_kernel(
    partners, v_own, v_before, v_after, p_own, p_before, p_after, out, split, source, target, total
):
    leaves, _, size = target.shape
    count = partners.shape[1]
    rhs = v_own.shape[0]
    own = p_own[...]
    top = jnp.max(own, axis=1, keepdims=True)
    bottom = jnp.min(own, axis=1, keepdims=True)
    centre = 0.5 * (top + bottom)
    wide = features(own, centre, False).astype(jnp.bfloat16)
    for leaf in range(leaves):
        target[leaf] = wide[:, leaf * size : (leaf + 1) * size]
    for block, (vectors, points) in enumerate(
        ((v_before, p_before), (v_own, p_own), (v_after, p_after))
    ):
        wide = features(points[...], centre, True)
        for leaf in range(leaves):
            cut = slice(leaf * size, (leaf + 1) * size)
            at = block * leaves + leaf
            source[at] = wide[:, cut].T.astype(jnp.bfloat16)
            high, low = halves(vectors[:, cut])
            split[at, :rhs] = high
            split[at, rhs:] = low

    def one_target(leaf, carry):
        here = target[leaf]
        total[...] = jnp.zeros_like(total)

        def one_partner(k, carry):
            at = partners[leaf, k]
            square = lax.dot_general(source[at], here, NN, preferred_element_type=jnp.float32)
            square = jnp.maximum(square, TINY)
            distance = square * lax.rsqrt(square)
            value = (distance + LOG2E) * jnp.exp2(-distance)
            high, low = halves(value)
            both = split[at]
            first = lax.dot_general(both, high, NN, preferred_element_type=jnp.float32)
            second = lax.dot_general(both[:rhs], low, NN, preferred_element_type=jnp.float32)
            total[:rhs] += first[:rhs] + second
            total[rhs:] += first[rhs:]
            return carry

        lax.fori_loop(0, count, one_partner, 0)
        start = pl.multiple_of(leaf * size, size)
        out[:, pl.ds(start, size)] = (total[:rhs] + total[rhs:]) * LN2
        return carry

    lax.fori_loop(0, leaves, one_target, 0)


def down_kernel(codes, *refs):
    slots = refs[:-11]
    near, basis, first, second, c_zero, c_one, c_two, out, table, fields, sems = refs[-11:]
    units = slots[0].shape[0]
    copies = []
    for i, slot in enumerate(slots):
        copies.append(
            pltpu.make_async_copy(slot, table.at[pl.ds(i * units, units)], sems.at[i])
        )
    for copy in copies:
        copy.start()
    for copy in copies:
        copy.wait()
    leaves, rank, size = basis.shape
    rhs = near.shape[0]
    lane = lax.broadcasted_iota(jnp.int32, (rhs, 2 * rank), 1)
    partner_count = codes.shape[1]

    def field(node, coupling):
        pieces = []
        for k in range(0, partner_count, 2):
            even, odd = codes[node, k], codes[node, k + 1]
            left = pltpu.roll(table[even // 2], (even % 2) * rank, 1)
            right = pltpu.roll(table[odd // 2], (1 - odd % 2) * rank, 1)
            pieces.append(jnp.where(lane < rank, left, right))
        return product(jnp.concatenate(pieces, axis=1), coupling, NT)

    def level(base, coupling):
        def step(i, carry):
            at = base + i
            even = field(2 * at, coupling[2 * i])
            odd = field(2 * at + 1, coupling[2 * i + 1])
            fields[at] = jnp.concatenate([even, odd], axis=1)
            return carry

        lax.fori_loop(0, coupling.shape[0] // 2, step, 0)

    level(0, c_zero)
    level(leaves // 2, c_one)
    level(leaves // 2 + leaves // 4, c_two)

    ones = []
    for p in range(leaves // 4):
        pair = fields[leaves // 2 + leaves // 4 + p // 2]
        top = pair[:, :rank] if p % 2 == 0 else pair[:, rank:]
        ones.append(fields[leaves // 2 + p] + product(top, second[p], NN))
    for p in range(leaves // 2):
        pair = ones[p // 2]
        top = pair[:, :rank] if p % 2 == 0 else pair[:, rank:]
        zeros = fields[p] + product(top, first[p], NN)
        for half in range(2):
            leaf = 2 * p + half
            low = zeros[:, :rank] if half == 0 else zeros[:, rank:]
            cut = slice(leaf * size, (leaf + 1) * size)
            out[:, cut] = near[:, cut] + product(low, basis[leaf], NN)


def whole_vmem(n):
    return [pl.BlockSpec(memory_space=pltpu.VMEM)] * n


def params():
    return pltpu.CompilerParams(vmem_limit_bytes=VMEM_LIMIT)


def on_device(
    devices,
    points,
    input_vectors,
    leaf_basis,
    transfer_one,
    transfer_two,
    coupling_zero,
    coupling_one,
    coupling_two,
    neighbour_leaves,
    far_zero,
    far_one,
    far_two,
):
    leaves, rank, size = leaf_basis.shape
    rhs = input_vectors.shape[0]
    me = lax.axis_index("leaf")
    up = [(i, i + 1) for i in range(devices - 1)]
    down = [(i + 1, i) for i in range(devices - 1)]
    v_before = lax.ppermute(input_vectors, "leaf", up)
    v_after = lax.ppermute(input_vectors, "leaf", down)
    p_before = lax.ppermute(points, "leaf", up)
    p_after = lax.ppermute(points, "leaf", down)

    units = leaves // 2 + leaves // 4 + leaves // 8
    coeffs = pl.pallas_call(
        up_kernel,
        out_shape=jax.ShapeDtypeStruct((units, rhs, 2 * rank), jnp.float32),
        in_specs=whole_vmem(4),
        out_specs=pl.BlockSpec(memory_space=pltpu.VMEM),
        compiler_params=params(),
        name="up",
    )(input_vectors, leaf_basis, transfer_one, transfer_two)

    lines = devices // 4

    def swap(value, line_step, row_flip, core_flip):
        pairs = []
        for i in range(devices):
            line, row, core = i // 4, i // 2 % 2, i % 2
            there = ((line + line_step) % lines * 2 + (row ^ row_flip)) * 2 + (core ^ core_flip)
            pairs.append((i, there))
        return lax.ppermute(value, "leaf", pairs)

    along = [coeffs] + [swap(coeffs, k, 0, 0) for k in range(1, lines)]
    across = [swap(value, 0, 1, 0) for value in along]
    near_side = along + across
    slots = near_side + [swap(value, 0, 0, 1) for value in near_side]

    first_leaf = (me - 1) * leaves
    near = pl.pallas_call(
        near_kernel,
        out_shape=jax.ShapeDtypeStruct(input_vectors.shape, jnp.float32),
        in_specs=[pl.BlockSpec(memory_space=pltpu.SMEM)] + whole_vmem(6),
        out_specs=pl.BlockSpec(memory_space=pltpu.VMEM),
        scratch_shapes=[
            pltpu.VMEM((3 * leaves, 2 * rhs, size), jnp.bfloat16),
            pltpu.VMEM((3 * leaves, size, 32), jnp.bfloat16),
            pltpu.VMEM((leaves, 32, size), jnp.bfloat16),
            pltpu.VMEM((2 * rhs, size), jnp.float32),
        ],
        compiler_params=params(),
        name="near",
    )(
        neighbour_leaves - first_leaf,
        input_vectors,
        v_before,
        v_after,
        points,
        p_before,
        p_after,
    )

    codes = []
    base = 0
    for partners, nodes in ((far_zero, leaves), (far_one, leaves // 2), (far_two, leaves // 4)):
        owner = partners // nodes
        local = partners % nodes
        step = (me // 4 - owner // 4 + lines) % lines
        row = (me // 2 + owner // 2) % 2
        core = (me + owner) % 2
        slot = (core * 2 + row) * lines + step
        codes.append((slot * units + base + local // 2) * 2 + local % 2)
        base += nodes // 2
    codes = jnp.concatenate(codes, axis=0)

    return pl.pallas_call(
        down_kernel,
        out_shape=jax.ShapeDtypeStruct(input_vectors.shape, jnp.float32),
        in_specs=[pl.BlockSpec(memory_space=pltpu.SMEM)]
        + [pl.BlockSpec(memory_space=pl.ANY)] * len(slots)
        + whole_vmem(7),
        out_specs=pl.BlockSpec(memory_space=pltpu.VMEM),
        scratch_shapes=[
            pltpu.VMEM((len(slots) * units, rhs, 2 * rank), jnp.float32),
            pltpu.VMEM((units, rhs, 2 * rank), jnp.float32),
            pltpu.SemaphoreType.DMA((len(slots),)),
        ],
        compiler_params=params(),
        name="down",
    )(
        codes,
        *slots,
        near,
        leaf_basis,
        transfer_one,
        transfer_two,
        coupling_zero,
        coupling_one,
        coupling_two,
    )


def solution(mesh):
    whole = ("groups", "leaf")
    columns, nodes, lists = P(None, whole), P(whole, None, None), P(whole, None)
    return jax.shard_map(
        functools.partial(on_device, mesh.shape["leaf"]),
        mesh=mesh,
        in_specs=(columns, columns) + (nodes,) * 6 + (lists,) * 4,
        out_specs=columns,
        check_vma=False,
    )
```

time: 272 us -> 231 us (0.85)
  the two profiles are of different devices: /device:TPU:9 before, /device:TPU:19 now
where the time goes in v1:
time: 231 us
  Pallas kernels  122 us (53%)
  starting transfers between devices  76.1 us (33%)
  waiting for transfers between devices  30.2 us (13%)
    pallas_call x1, Pallas kernels, on_device(): pl.pallas_call(near_kernel, out_shape=jax.ShapeDtypeStruct(input_vectors....  104 us
    ppermute x15, starting transfers between devices, swap(): return lax.ppermute(value, 'leaf', pairs)  35.4 us
    ppermute x1, starting transfers between devices, on_device(): p_after = lax.ppermute(points, 'leaf', down)  32.1 us
    ppermute x15, waiting for transfers between devices, swap(): return lax.ppermute(value, 'leaf', pairs)  23.1 us
    pallas_call x1, Pallas kernels, on_device(): pl.pallas_call(down_kernel, out_shape=jax.ShapeDtypeStruct(input_vectors....  14.4 us
    ppermute x1, waiting for transfers between devices, on_device(): p_before = lax.ppermute(points, 'leaf', up)  6.21 us
  transfers between devices with their start and end apart: 19, of which 4 were waited for; matrix products, arithmetic and copies ran while one was open for 1% of the time, Pallas kernels for 45%

profile of v1, /device:TPU:19, one launch (start us, length us, event | category | flops | bytes accessed | tf_op | source)
XLA Modules:
  0.0 231.1 jit_solution(1277917744987040094)
XLA Ops:
  0.0 3.6 %up.1.refs_0_ = f32[14,64,128]{2,1,0:T(8,128)} custom-call(f32[64,4096]{1,0:T(8,128)} %v_own.1, f32[16,64,256]{2,1,0:T(8,128)} %refs_17_.1, f32[8,64,128]{2,1,0:T(8,128)} %refs_18_.1, f32[4,64,128]{2,1,0:T(8,128)} %refs_19_.1), custom_call_target="tpu_custom_call" | custom-call | tf_op jit(solution)/shard_map/up/pallas_call | solution.py:224
  3.6 1.3 collective-permute-start
  5.0 1.1 collective-permute-start.2
  6.1 1.2 collective-permute-start.3
  7.3 3.7 %collective-permute-start.17 = (f32[3,4096]{1,0:T(4,128)S(1)}, f32[3,4096]{1,0:T(4,128)S(1)}, u32[]{:S(2)}, u32[]{:S(2)}) collective-permute-start(f32[3,4096]{1,0:T(4,128)S(1)} %copy-done.9), channel_id=1, source_target_pairs={{0,1},{1,2},{2,3},{3,4},{4,5},{5,6},{6,7},{7,8},{8,9},{9,10},{10,1... | collective-permute-start | bytes 147464 | tf_op jit(solution)/shard_map/ppermute | solution.py:220
  11.1 6.2 %collective-permute-done.17.p_before = f32[3,4096]{1,0:T(4,128)S(1)} collective-permute-done((f32[3,4096]{1,0:T(4,128)S(1)}, f32[3,4096]{1,0:T(4,128)S(1)}, u32[]{:S(2)}, u32[]{:S(2)}) %collective-permute-start.17) | collective-permute-done | bytes 49184 | tf_op jit(solution)/shard_map/ppermute | solution.py:220
  17.3 32.1 %collective-permute-start.18 = (f32[3,4096]{1,0:T(4,128)S(1)}, f32[3,4096]{1,0:T(4,128)S(1)}, u32[]{:S(2)}, u32[]{:S(2)}) collective-permute-start(f32[3,4096]{1,0:T(4,128)S(1)} %copy-done.9), channel_id=1, source_target_pairs={{1,0},{2,1},{3,2},{4,3},{5,4},{6,5},{7,6},{8,7},{9,8},{10,9},{11,1... | collective-permute-start | bytes 147464 | tf_op jit(solution)/shard_map/ppermute | solution.py:221
  49.4 0.9 collective-permute-done.18.p_after
  50.3 1.9 collective-permute-start.15
  52.2 2.9 %collective-permute-start.16 = (f32[64,4096]{1,0:T(8,128)S(1)}, f32[64,4096]{1,0:T(8,128)S(1)}, u32[]{:S(2)}, u32[]{:S(2)}) collective-permute-start(f32[64,4096]{1,0:T(8,128)S(1)} %copy-done), channel_id=1, source_target_pairs={{1,0},{2,1},{3,2},{4,3},{5,4},{6,5},{7,6},{8,7},{9,8},{10,9},{11,1... | collective-permute-start | bytes 3145736 | tf_op jit(solution)/shard_map/ppermute | solution.py:219
  55.2 2.7 %collective-permute-start.7 = (f32[14,64,128]{2,1,0:T(8,128)}, f32[14,64,128]{2,1,0:T(8,128)S(1)}, u32[]{:S(2)}, u32[]{:S(2)}) collective-permute-start(f32[14,64,128]{2,1,0:T(8,128)} %up.1.refs_0_), channel_id=1, source_target_pairs={{0,1},{1,0},{2,3},{3,2},{4,5},{5,4},{6,7},{7,6},{8,9},{9,8},{10,11... | collective-permute-start | bytes 1376264 | tf_op jit(solution)/shard_map/ppermute | solution.py:241
  57.9 1.5 collective-permute-start.5
  59.5 0.1 collective-permute-done.7.refs_8_
  59.6 23.0 %collective-permute-done.4.refs_5_ = f32[14,64,128]{2,1,0:T(8,128)S(1)} collective-permute-done((f32[14,64,128]{2,1,0:T(8,128)}, f32[14,64,128]{2,1,0:T(8,128)S(1)}, u32[]{:S(2)}, u32[]{:S(2)}) %collective-permute-start.4) | collective-permute-done | bytes 458784 | tf_op jit(solution)/shard_map/ppermute | solution.py:241
  82.6 16.7 %collective-permute-start.10 = (f32[14,64,128]{2,1,0:T(8,128)}, f32[14,64,128]{2,1,0:T(8,128)}, u32[]{:S(2)}, u32[]{:S(2)}) collective-permute-start(f32[14,64,128]{2,1,0:T(8,128)} %collective-permute-done.2.refs_3_), channel_id=1, source_target_pairs={{0,1},{1,0},{2,3},{3,2},{4,5},{5,4},{6,7},{7,6},{8,9},{9,8},{10,11... | collective-permute-start | bytes 1376264 | tf_op jit(solution)/shard_map/ppermute | solution.py:241
  99.3 4.9 %collective-permute-start.8 = (f32[14,64,128]{2,1,0:T(8,128)}, f32[14,64,128]{2,1,0:T(8,128)}, u32[]{:S(2)}, u32[]{:S(2)}) collective-permute-start(f32[14,64,128]{2,1,0:T(8,128)} %collective-permute-done.refs_1_), channel_id=1, source_target_pairs={{0,1},{1,0},{2,3},{3,2},{4,5},{5,4},{6,7},{7,6},{8,9},{9,8},{10,11... | collective-permute-start | bytes 1376264 | tf_op jit(solution)/shard_map/ppermute | solution.py:241
  104.4 4.8 %collective-permute-start.9 = (f32[14,64,128]{2,1,0:T(8,128)}, f32[14,64,128]{2,1,0:T(8,128)}, u32[]{:S(2)}, u32[]{:S(2)}) collective-permute-start(f32[14,64,128]{2,1,0:T(8,128)} %copy-done.3), channel_id=1, source_target_pairs={{0,1},{1,0},{2,3},{3,2},{4,5},{5,4},{6,7},{7,6},{8,9},{9,8},{10,11... | collective-permute-start | bytes 1376264 | tf_op jit(solution)/shard_map/ppermute | solution.py:241
  109.2 0.5 collective-permute-start.12
  109.8 0.4 collective-permute-start.14
  110.3 0.7 copy.25.codes
  111.0 0.6 broadcast_subtract_fusion.partners
  111.6 104.2 %near.1.refs_16_ = f32[64,4096]{1,0:T(8,128)} custom-call(s32[16,16]{1,0:T(8,128)} %broadcast_subtract_fusion.partners, f32[64,4096]{1,0:T(8,128)} %v_own.1, f32[64,4096]{1,0:T(8,128)} %copy-done.1, f32[64,4096]{1,0:T(8,128)} %copy-done.2, f32[3,4096]{1,0:T(4,128)} %p_own.1, f32[3,4096]{1,0:T(4,128)} %copy-done.10, f32[3,4096]{1,0:T(4,128)} %copy-done.11), custom_call_target="tpu_custom_call" | custom-call | tf_op jit(solution)/shard_map/near/pallas_call | solution.py:249
  215.9 0.8 copy-done.8
  216.7 14.4 %down.1 = f32[64,4096]{1,0:T(8,128)} custom-call(s32[28,8]{1,0:T(8,128)} %copy.25.codes, f32[14,64,128]{2,1,0:T(8,128)} %up.1.refs_0_, f32[14,64,128]{2,1,0:T(8,128)} %collective-permute-done.refs_1_, f32[14,64,128]{2,1,0:T(8,128)} %copy-done.3, f32[14,64,128]{2,1,0:T(8,128)} %collective-permute-done.2.refs_3_, f32[14,64,128]{2,1,0:T(8,128)} %copy-done.4, ...), custom_call_target="tpu_custom_call" | custom-call | tf_op jit(solution)/shard_map/down/pallas_call | solution.py:285
  (57 shorter events, 0.6 us)
Async XLA Ops:
  0.0 104.2 %copy-start.13 = (s32[8,8]{1,0:T(8,128)S(1)}, s32[8,8]{1,0:T(8,128)}, u32[]{:S(2)}) copy-start(s32[8,8]{1,0:T(8,128)} %param.22) | copy-start | bytes 772
  0.0 104.3 %copy-start.15 = (s32[4,8]{1,0:T(4,128)S(1)}, s32[4,8]{1,0:T(4,128)}, u32[]{:S(2)}) copy-start(s32[4,8]{1,0:T(4,128)} %param.23) | copy-start | bytes 388
  0.0 104.3 %copy-start.14 = (s32[16,8]{0,1:T(8,128)S(1)}, s32[16,8]{0,1:T(8,128)}, u32[]{:S(2)}) copy-start(s32[16,8]{0,1:T(8,128)} %param.21) | copy-start | bytes 1540
  0.0 111.0 %copy-start.12 = (s32[16,16]{1,0:T(8,128)S(1)}, s32[16,16]{1,0:T(8,128)}, u32[]{:S(2)}) copy-start(s32[16,16]{1,0:T(8,128)} %param.20) | copy-start | bytes 3076
  3.6 48.6 %collective-permute-start = (f32[14,64,128]{2,1,0:T(8,128)}, f32[14,64,128]{2,1,0:T(8,128)}, u32[]{:S(2)}, u32[]{:S(2)}) collective-permute-start(f32[14,64,128]{2,1,0:T(8,128)} %up.1.refs_0_), channel_id=1, source_target_pairs={{0,4},{1,5},{2,6},{3,7},{4,8},{5,9},{6,10},{7,11},{8,12},{9,13},{1... | collective-permute-start | bytes 1376264 | tf_op jit(solution)/shard_map/ppermute | solution.py:241
  4.9 50.2 %collective-permute-start.1 = (f32[14,64,128]{2,1,0:T(8,128)}, f32[14,64,128]{2,1,0:T(8,128)S(1)}, u32[]{:S(2)}, u32[]{:S(2)}) collective-permute-start(f32[14,64,128]{2,1,0:T(8,128)} %up.1.refs_0_), channel_id=1, source_target_pairs={{0,8},{1,9},{2,10},{3,11},{4,12},{5,13},{6,14},{7,15},{8,0},{9,1},... | collective-permute-start | bytes 1376264 | tf_op jit(solution)/shard_map/ppermute | solution.py:241
  5.0 53.0 %collective-permute-start.2 = (f32[14,64,128]{2,1,0:T(8,128)}, f32[14,64,128]{2,1,0:T(8,128)}, u32[]{:S(2)}, u32[]{:S(2)}) collective-permute-start(f32[14,64,128]{2,1,0:T(8,128)} %up.1.refs_0_), channel_id=1, source_target_pairs={{0,12},{1,13},{2,14},{3,15},{4,0},{5,1},{6,2},{7,3},{8,4},{9,5},{1... | collective-permute-start | bytes 1376264 | tf_op jit(solution)/shard_map/ppermute | solution.py:241
  6.1 51.8 %collective-permute-start.3 = (f32[14,64,128]{2,1,0:T(8,128)}, f32[14,64,128]{2,1,0:T(8,128)S(1)}, u32[]{:S(2)}, u32[]{:S(2)}) collective-permute-start(f32[14,64,128]{2,1,0:T(8,128)} %up.1.refs_0_), channel_id=1, source_target_pairs={{0,2},{1,3},{2,0},{3,1},{4,6},{5,7},{6,4},{7,5},{8,10},{9,11},{10,... | collective-permute-start | bytes 1376264 | tf_op jit(solution)/shard_map/ppermute | solution.py:241
  7.3 10.0 %collective-permute-start.17 = (f32[3,4096]{1,0:T(4,128)S(1)}, f32[3,4096]{1,0:T(4,128)S(1)}, u32[]{:S(2)}, u32[]{:S(2)}) collective-permute-start(f32[3,4096]{1,0:T(4,128)S(1)} %copy-done.9), channel_id=1, source_target_pairs={{0,1},{1,2},{2,3},{3,4},{4,5},{5,6},{6,7},{7,8},{8,9},{9,10},{10,1... | collective-permute-start | bytes 147464 | tf_op jit(solution)/shard_map/ppermute | solution.py:220
  17.3 94.3 %copy-start.10 = (f32[3,4096]{1,0:T(4,128)}, f32[3,4096]{1,0:T(4,128)S(1)}, u32[]{:S(2)}) copy-start(f32[3,4096]{1,0:T(4,128)S(1)} %collective-permute-done.17.p_before) | copy-start | bytes 147460
  17.3 33.0 %collective-permute-start.18 = (f32[3,4096]{1,0:T(4,128)S(1)}, f32[3,4096]{1,0:T(4,128)S(1)}, u32[]{:S(2)}, u32[]{:S(2)}) collective-permute-start(f32[3,4096]{1,0:T(4,128)S(1)} %copy-done.9), channel_id=1, source_target_pairs={{1,0},{2,1},{3,2},{4,3},{5,4},{6,5},{7,6},{8,7},{9,8},{10,9},{11,1... | collective-permute-start | bytes 147464 | tf_op jit(solution)/shard_map/ppermute | solution.py:221
  50.3 59.4 %collective-permute-start.15 = (f32[64,4096]{1,0:T(8,128)S(1)}, f32[64,4096]{1,0:T(8,128)S(1)}, u32[]{:S(2)}, u32[]{:S(2)}) collective-permute-start(f32[64,4096]{1,0:T(8,128)S(1)} %copy-done), channel_id=1, source_target_pairs={{0,1},{1,2},{2,3},{3,4},{4,5},{5,6},{6,7},{7,8},{8,9},{9,10},{10,1... | collective-permute-start | bytes 3145736 | tf_op jit(solution)/shard_map/ppermute | solution.py:218
  52.2 57.6 %collective-permute-start.16 = (f32[64,4096]{1,0:T(8,128)S(1)}, f32[64,4096]{1,0:T(8,128)S(1)}, u32[]{:S(2)}, u32[]{:S(2)}) collective-permute-start(f32[64,4096]{1,0:T(8,128)S(1)} %copy-done), channel_id=1, source_target_pairs={{1,0},{2,1},{3,2},{4,3},{5,4},{6,5},{7,6},{8,7},{9,8},{10,9},{11,1... | collective-permute-start | bytes 3145736 | tf_op jit(solution)/shard_map/ppermute | solution.py:219
  55.2 4.4 %collective-permute-start.7 = (f32[14,64,128]{2,1,0:T(8,128)}, f32[14,64,128]{2,1,0:T(8,128)S(1)}, u32[]{:S(2)}, u32[]{:S(2)}) collective-permute-start(f32[14,64,128]{2,1,0:T(8,128)} %up.1.refs_0_), channel_id=1, source_target_pairs={{0,1},{1,0},{2,3},{3,2},{4,5},{5,4},{6,7},{7,6},{8,9},{9,8},{10,11... | collective-permute-start | bytes 1376264 | tf_op jit(solution)/shard_map/ppermute | solution.py:241
  57.9 24.7 %collective-permute-start.4 = (f32[14,64,128]{2,1,0:T(8,128)}, f32[14,64,128]{2,1,0:T(8,128)S(1)}, u32[]{:S(2)}, u32[]{:S(2)}) collective-permute-start(f32[14,64,128]{2,1,0:T(8,128)} %collective-permute-done.refs_1_), channel_id=1, source_target_pairs={{0,2},{1,3},{2,0},{3,1},{4,6},{5,7},{6,4},{7,5},{8,10},{9,11},{10,... | collective-permute-start | bytes 1376264 | tf_op jit(solution)/shard_map/ppermute | solution.py:241
  57.9 41.3 %collective-permute-start.5 = (f32[14,64,128]{2,1,0:T(8,128)S(1)}, f32[14,64,128]{2,1,0:T(8,128)S(1)}, u32[]{:S(2)}, u32[]{:S(2)}) collective-permute-start(f32[14,64,128]{2,1,0:T(8,128)S(1)} %collective-permute-done.1.refs_2_), channel_id=1, source_target_pairs={{0,2},{1,3},{2,0},{3,1},{4,6},{5,7},{6,4},{7,5},{8,10},{9,11},{10,... | collective-permute-start | bytes 1376264 | tf_op jit(solution)/shard_map/ppermute | solution.py:241
  59.6 44.8 %collective-permute-start.6 = (f32[14,64,128]{2,1,0:T(8,128)}, f32[14,64,128]{2,1,0:T(8,128)}, u32[]{:S(2)}, u32[]{:S(2)}) collective-permute-start(f32[14,64,128]{2,1,0:T(8,128)} %collective-permute-done.2.refs_3_), channel_id=1, source_target_pairs={{0,2},{1,3},{2,0},{3,1},{4,6},{5,7},{6,4},{7,5},{8,10},{9,11},{10,... | collective-permute-start | bytes 1376264 | tf_op jit(solution)/shard_map/ppermute | solution.py:241
  82.6 26.6 %collective-permute-start.10 = (f32[14,64,128]{2,1,0:T(8,128)}, f32[14,64,128]{2,1,0:T(8,128)}, u32[]{:S(2)}, u32[]{:S(2)}) collective-permute-start(f32[14,64,128]{2,1,0:T(8,128)} %collective-permute-done.2.refs_3_), channel_id=1, source_target_pairs={{0,1},{1,0},{2,3},{3,2},{4,5},{5,4},{6,7},{7,6},{8,9},{9,8},{10,11... | collective-permute-start | bytes 1376264 | tf_op jit(solution)/shard_map/ppermute | solution.py:241
  99.3 9.9 %collective-permute-start.8 = (f32[14,64,128]{2,1,0:T(8,128)}, f32[14,64,128]{2,1,0:T(8,128)}, u32[]{:S(2)}, u32[]{:S(2)}) collective-permute-start(f32[14,64,128]{2,1,0:T(8,128)} %collective-permute-done.refs_1_), channel_id=1, source_target_pairs={{0,1},{1,0},{2,3},{3,2},{4,5},{5,4},{6,7},{7,6},{8,9},{9,8},{10,11... | collective-permute-start | bytes 1376264 | tf_op jit(solution)/shard_map/ppermute | solution.py:241
  104.4 111.5 %collective-permute-start.9 = (f32[14,64,128]{2,1,0:T(8,128)}, f32[14,64,128]{2,1,0:T(8,128)}, u32[]{:S(2)}, u32[]{:S(2)}) collective-permute-start(f32[14,64,128]{2,1,0:T(8,128)} %copy-done.3), channel_id=1, source_target_pairs={{0,1},{1,0},{2,3},{3,2},{4,5},{5,4},{6,7},{7,6},{8,9},{9,8},{10,11... | collective-permute-start | bytes 1376264 | tf_op jit(solution)/shard_map/ppermute | solution.py:241
  109.2 106.7 %collective-permute-start.11 = (f32[14,64,128]{2,1,0:T(8,128)}, f32[14,64,128]{2,1,0:T(8,128)}, u32[]{:S(2)}, u32[]{:S(2)}) collective-permute-start(f32[14,64,128]{2,1,0:T(8,128)} %copy-done.4), channel_id=1, source_target_pairs={{0,1},{1,0},{2,3},{3,2},{4,5},{5,4},{6,7},{7,6},{8,9},{9,8},{10,11... | collective-permute-start | bytes 1376264 | tf_op jit(solution)/shard_map/ppermute | solution.py:241
  109.2 106.7 %collective-permute-start.12 = (f32[14,64,128]{2,1,0:T(8,128)}, f32[14,64,128]{2,1,0:T(8,128)}, u32[]{:S(2)}, u32[]{:S(2)}) collective-permute-start(f32[14,64,128]{2,1,0:T(8,128)} %copy-done.6), channel_id=1, source_target_pairs={{0,1},{1,0},{2,3},{3,2},{4,5},{5,4},{6,7},{7,6},{8,9},{9,8},{10,11... | collective-permute-start | bytes 1376264 | tf_op jit(solution)/shard_map/ppermute | solution.py:241
  109.7 106.2 %collective-permute-start.13 = (f32[14,64,128]{2,1,0:T(8,128)}, f32[14,64,128]{2,1,0:T(8,128)}, u32[]{:S(2)}, u32[]{:S(2)}) collective-permute-start(f32[14,64,128]{2,1,0:T(8,128)} %copy-done.7), channel_id=1, source_target_pairs={{0,1},{1,0},{2,3},{3,2},{4,5},{5,4},{6,7},{7,6},{8,9},{9,8},{10,11... | collective-permute-start | bytes 1376264 | tf_op jit(solution)/shard_map/ppermute | solution.py:241
  109.8 106.1 %collective-permute-start.14 = (f32[14,64,128]{2,1,0:T(8,128)}, f32[14,64,128]{2,1,0:T(8,128)S(1)}, u32[]{:S(2)}, u32[]{:S(2)}) collective-permute-start(f32[14,64,128]{2,1,0:T(8,128)} %collective-permute-done.6.refs_7_), channel_id=1, source_target_pairs={{0,1},{1,0},{2,3},{3,2},{4,5},{5,4},{6,7},{7,6},{8,9},{9,8},{10,11... | collective-permute-start | bytes 1376264 | tf_op jit(solution)/shard_map/ppermute | solution.py:241
  (11 other events, 238.8 us)

commit v2 on v1

v2 whole, which is shorter than its diff:
```python
import functools
import math

import jax
import jax.numpy as jnp
from jax import lax
from jax.experimental import pallas as pl
from jax.experimental.pallas import tpu as pltpu
from jax.sharding import PartitionSpec as P

LOG2E = math.log2(math.e)
LN2 = math.log(2.0)
SCALE = math.sqrt(3.0) / 0.05 * LOG2E
TINY = 1e-10
NN = (((1,), (0,)), ((), ()))
NT = (((1,), (1,)), ((), ()))
GROUP = 8
NEAR_WORK = 10**10
OWN_WORK = 10**6
DOWN_MEBIBYTES = 56


def halves(value):
    high = value.astype(jnp.bfloat16)
    low = (value - high.astype(jnp.float32)).astype(jnp.bfloat16)
    return high, low


def product(left, right, dims):
    left_high, left_low = halves(left)
    right_high, right_low = halves(right)
    dot = functools.partial(lax.dot_general, preferred_element_type=jnp.float32)
    return (
        dot(left_high, right_high, dims)
        + dot(left_high, right_low, dims)
        + dot(left_low, right_high, dims)
    )


def up_kernel(neighbours, vectors, basis, first, second, _, out, lists):
    me = lax.axis_index("leaf")
    leaves, _, size = basis.shape
    rank = basis.shape[1]
    pairs = []
    for pair in range(leaves // 2):
        both = []
        for leaf in (2 * pair, 2 * pair + 1):
            columns = vectors[:, leaf * size : (leaf + 1) * size]
            both.append(product(columns, basis[leaf], NT))
        pairs.append(jnp.concatenate(both, axis=1))
        out[pair] = pairs[pair]
    base = len(pairs)
    for transfer in (first, second):
        nodes = [product(pairs[i], transfer[i], NT) for i in range(len(pairs))]
        pairs = [
            jnp.concatenate(nodes[2 * i : 2 * i + 2], axis=1) for i in range(len(nodes) // 2)
        ]
        for i, pair in enumerate(pairs):
            out[base + i] = pair
        base += len(pairs)
    pair_lists(neighbours[...] - (me - 1) * leaves, leaves, lists)


def pick_kernel(lines, leaves, units, far_zero, far_one, far_two, codes):
    me = lax.axis_index("leaf")
    unit, row = 0, 0
    for far, nodes in ((far_zero, leaves), (far_one, leaves // 2), (far_two, leaves // 4)):
        owner = far[...] // nodes
        local = far[...] % nodes
        step = (me // 4 - owner // 4 + lines) % lines
        across = (me // 2 + owner // 2) % 2
        core = (me + owner) % 2
        slot = (core * 2 + across) * lines + step
        codes[row : row + nodes] = (slot * units + unit + local // 2) * 2 + local % 2
        unit += nodes // 2
        row += nodes


def thirds(value):
    high = value.astype(jnp.bfloat16).astype(jnp.float32)
    rest = value - high
    middle = rest.astype(jnp.bfloat16).astype(jnp.float32)
    low = (rest - middle).astype(jnp.bfloat16).astype(jnp.float32)
    return high, middle, low


def features(points, centre, source):
    scaled = (points - centre) * SCALE
    high, middle, low = thirds(scaled)
    square = jnp.sum(scaled * scaled, axis=0, keepdims=True)
    parts = jnp.concatenate(thirds(square), axis=0)
    ones = jnp.ones_like(parts)
    pad = jnp.zeros((8, points.shape[1]), jnp.float32)
    if source:
        rows = [high, high, middle, middle, high, low, parts, ones, pad]
    else:
        rows = [-2.0 * v for v in (high, middle, high, middle, low, high)]
        rows += [ones, parts, pad]
    return jnp.concatenate(rows, axis=0)


def pair_lists(relative, leaves, out):
    targets, count = relative.shape
    ids = relative.astype(jnp.float32)
    column = lax.broadcasted_iota(jnp.int32, (targets, count), 1)
    row = lax.broadcasted_iota(jnp.int32, (targets, count), 0)
    times = jnp.zeros((targets, count), jnp.float32)
    earlier = jnp.zeros((targets, count), jnp.float32)
    for k in range(count):
        same = jnp.where(ids == ids[:, k : k + 1], 1.0, 0.0)
        times += same
        earlier += jnp.where(column > k, same, 0.0)
    before = jnp.where(
        lax.broadcasted_iota(jnp.int32, (count, count), 0)
        < lax.broadcasted_iota(jnp.int32, (count, count), 1),
        1.0,
        0.0,
    )
    above = jnp.where(
        lax.broadcasted_iota(jnp.int32, (targets, targets), 1)
        < lax.broadcasted_iota(jnp.int32, (targets, targets), 0),
        1.0,
        0.0,
    )
    width = targets * count
    place = lax.broadcasted_iota(jnp.int32, (targets, width), 1).astype(jnp.float32)
    for i in range(3):
        source = relative - i * leaves
        keep = jnp.where((source >= 0) & (source < leaves) & (earlier == 0.0), 1.0, 0.0)
        rank = lax.dot_general(keep, before, NN, preferred_element_type=jnp.float32)
        sums = jnp.sum(keep, axis=1, keepdims=True)
        wide = jnp.broadcast_to(sums, (targets, count))
        rank += lax.dot_general(above, wide, NN, preferred_element_type=jnp.float32)
        code = (times * targets + row.astype(jnp.float32)) * leaves
        code = (code + source.astype(jnp.float32)) * keep
        rank = jnp.where(keep > 0.0, rank, -1.0)
        flat = jnp.zeros((targets, width), jnp.float32)
        for k in range(count):
            flat += jnp.where(rank[:, k : k + 1] == place, code[:, k : k + 1], 0.0)
        out[i : i + 1] = jnp.sum(flat, axis=0, keepdims=True).astype(jnp.int32)
        total = jnp.sum(sums, axis=0, keepdims=True)
        out[i + 3 : i + 4] = jnp.broadcast_to(total, (1, width)).astype(jnp.int32)


def near_kernel(which, leaves, lists, p_own, block, *refs):
    so_far = None if which == 1 else refs[0]
    out, split, source, target, total = refs[-5:]
    rhs, size = split.shape[1] // 2, split.shape[2]
    own = p_own[...]
    top = jnp.max(own, axis=1, keepdims=True)
    bottom = jnp.min(own, axis=1, keepdims=True)
    centre = 0.5 * (top + bottom)
    wide = features(own, centre, False).astype(jnp.bfloat16)
    there = features(block[rhs : rhs + 3], centre, True)
    for leaf in range(leaves):
        cut = slice(leaf * size, (leaf + 1) * size)
        target[leaf] = wide[:, cut]
        total[leaf] = jnp.zeros(total.shape[1:], jnp.float32)
        source[leaf] = there[:, cut].T.astype(jnp.bfloat16)
        high, low = halves(block[:rhs, cut])
        split[leaf, :rhs] = high
        split[leaf, rhs:] = low

    dot = functools.partial(lax.dot_general, preferred_element_type=jnp.float32)

    def group(step, carry):
        for i in range(GROUP):
            code = lists[which, step * GROUP + i]
            at = code % leaves
            rest = code // leaves
            into = rest % leaves
            times = (rest // leaves).astype(jnp.float32)
            square = jnp.maximum(dot(source[at], target[into], NN), TINY)
            distance = square * lax.rsqrt(square)
            high, low = halves((distance + LOG2E) * jnp.exp2(-distance))
            both = split[at]
            total[into] += (dot(both, high, NN) + dot(both, low, NN)) * times
        return carry

    lax.fori_loop(0, (lists[which + 3, 0] + GROUP - 1) // GROUP, group, 0)
    for leaf in range(leaves):
        cut = slice(leaf * size, (leaf + 1) * size)
        value = (total[leaf, :rhs] + total[leaf, rhs:]) * LN2
        out[:, cut] = value if so_far is None else so_far[:, cut] + value


def down_kernel(codes, *refs):
    slots = refs[:-17]
    sources, out = refs[-17:-10], refs[-10]
    table, fields, *held, sems = refs[-9:]
    second, c_two, c_one, c_zero, first, basis = held
    units = slots[0].shape[0]
    targets = [table.at[pl.ds(i * units, units)] for i in range(len(slots))]
    targets += held + [out]
    copies = [
        pltpu.make_async_copy(source, target, sems.at[i])
        for i, (source, target) in enumerate(zip(slots + sources, targets))
    ]
    for copy in copies:
        copy.start()
    for copy in copies[: len(slots) + 2]:
        copy.wait()
    leaves, rank, size = basis.shape
    rhs = out.shape[0]
    lane = lax.broadcasted_iota(jnp.int32, (rhs, 2 * rank), 1)
    partner_count = codes.shape[1]

    def field(node, coupling):
        pieces = []
        for k in range(0, partner_count, 2):
            even, odd = codes[node, k], codes[node, k + 1]
            left = pltpu.roll(table[even // 2], (even % 2) * rank, 1)
            right = pltpu.roll(table[odd // 2], (1 - odd % 2) * rank, 1)
            pieces.append(jnp.where(lane < rank, left, right))
        return product(jnp.concatenate(pieces, axis=1), coupling, NT)

    def level(base, coupling):
        def step(i, carry):
            for j in range(2):
                at = 2 * i + j
                even = field(2 * (base + at), coupling[2 * at])
                odd = field(2 * (base + at) + 1, coupling[2 * at + 1])
                fields[base + at] = jnp.concatenate([even, odd], axis=1)
            return carry

        lax.fori_loop(0, coupling.shape[0] // 4, step, 0)

    level(leaves // 2 + leaves // 4, c_two)
    copies[len(slots) + 2].wait()
    level(leaves // 2, c_one)
    copies[len(slots) + 3].wait()
    level(0, c_zero)
    for copy in copies[len(slots) + 4 :]:
        copy.wait()

    ones = []
    for p in range(leaves // 4):
        pair = fields[leaves // 2 + leaves // 4 + p // 2]
        top = pair[:, :rank] if p % 2 == 0 else pair[:, rank:]
        ones.append(fields[leaves // 2 + p] + product(top, second[p], NN))
    for p in range(leaves // 2):
        pair = ones[p // 2]
        top = pair[:, :rank] if p % 2 == 0 else pair[:, rank:]
        zeros = fields[p] + product(top, first[p], NN)
        for half in range(2):
            leaf = 2 * p + half
            low = zeros[:, :rank] if half == 0 else zeros[:, rank:]
            cut = slice(leaf * size, (leaf + 1) * size)
            out[:, cut] += product(low, basis[leaf], NN)


def whole_vmem(n):
    return [pl.BlockSpec(memory_space=pltpu.VMEM)] * n


def params(mebibytes):
    return pltpu.CompilerParams(vmem_limit_bytes=mebibytes * 2**20)


def on_device(
    devices,
    points,
    input_vectors,
    leaf_basis,
    transfer_one,
    transfer_two,
    coupling_zero,
    coupling_one,
    coupling_two,
    neighbour_leaves,
    far_zero,
    far_one,
    far_two,
):
    leaves, rank, size = leaf_basis.shape
    rhs = input_vectors.shape[0]
    tie = lax.optimization_barrier
    before = [(i, i + 1) for i in range(devices - 1)]
    after = [(i + 1, i) for i in range(devices - 1)]
    stacked = jnp.concatenate([input_vectors, points], axis=0)
    from_before = lax.ppermute(stacked, "leaf", before)
    from_after = lax.ppermute(stacked, "leaf", after)

    lines = devices // 4

    def swap(value, line_step, row_flip, core_flip):
        pairs = []
        for i in range(devices):
            line, row, core = i // 4, i // 2 % 2, i % 2
            there = ((line + line_step) % lines * 2 + (row ^ row_flip)) * 2 + (core ^ core_flip)
            pairs.append((i, there))
        return lax.ppermute(value, "leaf", pairs)

    units = leaves // 2 + leaves // 4 + leaves // 8
    nodes = leaves + leaves // 2 + leaves // 4
    near_count, far_count = neighbour_leaves.shape[1], far_zero.shape[1]
    coeffs, lists = pl.pallas_call(
        up_kernel,
        out_shape=(
            jax.ShapeDtypeStruct((units, rhs, 2 * rank), jnp.float32),
            jax.ShapeDtypeStruct((6, leaves * near_count), jnp.int32),
        ),
        in_specs=whole_vmem(5) + [pl.BlockSpec(memory_space=pl.ANY)],
        out_specs=tuple(whole_vmem(2)),
        compiler_params=params(12),
        name="up",
    )(neighbour_leaves, input_vectors, leaf_basis, transfer_one, transfer_two, stacked)
    codes = pl.pallas_call(
        functools.partial(pick_kernel, lines, leaves, units),
        out_shape=jax.ShapeDtypeStruct((nodes, far_count), jnp.int32),
        in_specs=whole_vmem(3),
        out_specs=pl.BlockSpec(memory_space=pltpu.VMEM),
        compiler_params=params(2),
        name="picks",
    )(far_zero, far_one, far_two)

    def near_field(which, operand, work, near, *later):
        operands = (operand,) if near is None else (operand, near)
        return pl.pallas_call(
            functools.partial(near_kernel, which, leaves),
            out_shape=jax.ShapeDtypeStruct(input_vectors.shape, jnp.float32),
            in_specs=[pl.BlockSpec(memory_space=pltpu.SMEM)]
            + whole_vmem(1 + len(operands))
            + [pl.BlockSpec(memory_space=pl.ANY)] * len(later),
            out_specs=pl.BlockSpec(memory_space=pltpu.VMEM),
            scratch_shapes=[
                pltpu.VMEM((leaves, 2 * rhs, size), jnp.bfloat16),
                pltpu.VMEM((leaves, size, 32), jnp.bfloat16),
                pltpu.VMEM((leaves, 32, size), jnp.bfloat16),
                pltpu.VMEM((leaves, 2 * rhs, size), jnp.float32),
            ],
            cost_estimate=pl.CostEstimate(
                flops=work, bytes_accessed=3 * 2**20, transcendentals=0
            ),
            compiler_params=params(16),
            name=("near_before", "near_own", "near_after")[which],
        )(lists, points, *operands, *later)

    far_end = lines - 1
    held = {(0, 0): coeffs}
    for step, towards in {1: 1, far_end: -1}.items():
        held[0, step] = swap(coeffs, towards, 0, 0)
    held[1, 0] = swap(coeffs, 0, 1, 0)
    near = near_field(1, stacked, OWN_WORK, None)
    held, near = tie((held, near))
    middle = (lines + 1) // 2
    for step in range(2, middle + 1):
        if (0, step) not in held:
            held[0, step] = swap(held[0, step - 1], 1, 0, 0)
    for step in range(far_end - 1, middle, -1):
        held[0, step] = swap(held[0, step + 1], -1, 0, 0)
    if far_end > 1:
        held[1, far_end] = swap(held[0, far_end], 0, 1, 0)
    ends = [held[0, step] for step in sorted({1, far_end})]
    near = near_field(0, from_before, NEAR_WORK, near, from_after, *ends)
    along, near = tie(([held[0, step] for step in range(lines)], near))
    if (1, 1) not in held:
        behind, _ = tie((held[1, 0], along))
        held[1, 1] = swap(behind, 1, 0, 0)
    for step in range(2, far_end):
        held[1, step] = swap(along[step], 0, 1, 0)
    early = {(0, step): value for step, value in enumerate(along)}
    early[1, 0], near = tie((held[1, 0], near))
    across = {key: swap(value, 0, 0, 1) for key, value in early.items()}
    near = near_field(2, from_after, NEAR_WORK, near, *along[2:far_end])
    late = {key: value for key, value in held.items() if key not in early}
    late, near = tie((late, near))
    across.update({key: swap(value, 0, 0, 1) for key, value in late.items()})
    order = [(row, step) for row in range(2) for step in range(lines)]
    slots = [{**early, **late}[key] for key in order] + [across[key] for key in order]

    operands = (
        transfer_two,
        coupling_two,
        coupling_one,
        coupling_zero,
        transfer_one,
        leaf_basis,
    )
    copied = len(slots) + len(operands) + 1
    return pl.pallas_call(
        down_kernel,
        out_shape=jax.ShapeDtypeStruct(input_vectors.shape, jnp.float32),
        in_specs=[pl.BlockSpec(memory_space=pltpu.SMEM)]
        + [pl.BlockSpec(memory_space=pl.ANY)] * copied,
        out_specs=pl.BlockSpec(memory_space=pltpu.VMEM),
        scratch_shapes=[
            pltpu.VMEM((devices * units, rhs, 2 * rank), jnp.float32),
            pltpu.VMEM((units, rhs, 2 * rank), jnp.float32),
        ]
        + [pltpu.VMEM(operand.shape, jnp.float32) for operand in operands]
        + [pltpu.SemaphoreType.DMA((copied,))],
        compiler_params=params(DOWN_MEBIBYTES),
        name="down",
    )(codes, *slots, *operands, near)


def solution(mesh):
    whole = ("groups", "leaf")
    columns, nodes, lists = P(None, whole), P(whole, None, None), P(whole, None)
    return jax.shard_map(
        functools.partial(on_device, mesh.shape["leaf"]),
        mesh=mesh,
        in_specs=(columns, columns) + (nodes,) * 6 + (lists,) * 4,
        out_specs=columns,
        check_vma=False,
    )
```

time: 231 us -> 89.7 us (0.39)
  the two profiles are of different devices: /device:TPU:19 before, /device:TPU:0 now
where the time goes in v2:
time: 89.7 us; the launch traced here: 89.5 us
  Pallas kernels  37.8 us (42%)
  waiting for transfers between devices  28.5 us (32%)
  starting transfers between devices  15.9 us (18%)
  local copies, waits for them, and re-layouts  6.92 us (8%)
    ppermute x15, waiting for transfers between devices, swap(): return lax.ppermute(value, 'leaf', pairs)  28.5 us
    pallas_call x3, Pallas kernels, near_field(): pl.pallas_call(functools.partial(near_kernel, which, leaves), out_shape=j...  25.4 us
    ppermute x15, starting transfers between devices, swap(): return lax.ppermute(value, 'leaf', pairs)  11.5 us
    pallas_call x1, Pallas kernels, on_device(): pl.pallas_call(down_kernel, out_shape=jax.ShapeDtypeStruct(input_vectors....  11 us
    unnamed x46, local copies, waits for them, and re-layouts  6.06 us
    ppermute x1, starting transfers between devices, on_device(): from_before = lax.ppermute(stacked, 'leaf', before)  3.11 us
  transfers between devices with their start and end apart: 17, of which 9 were waited for; matrix products, arithmetic and copies ran while one was open for 0% of the time, Pallas kernels for 30%

profile of v2, /device:TPU:0, one launch (start us, length us, event | category | flops | bytes accessed | tf_op | source)
XLA Modules:
  0.0 89.5 jit_solution(12051153887402651856)
XLA Ops:
  0.0 1.4 %constant_dynamic-update-slice_fusion.1 = f32[67,4096]{1,0:T(8,128)S(1)} fusion(f32[64,4096]{1,0:T(8,128)} %vectors.1), kind=kLoop, calls=%fused_computation.1 | loop fusion | bytes 2097152
  1.5 0.9 constant_dynamic-update-slice_fusion._.block
  2.3 1.3 %collective-permute-start.5 = (f32[67,4096]{1,0:T(8,128)S(1)}, f32[67,4096]{1,0:T(8,128)S(1)}, u32[]{:S(2)}, u32[]{:S(2)}) collective-permute-start(f32[67,4096]{1,0:T(8,128)S(1)} %constant_dynamic-update-slice_fusion._.block), channel_id=1, source_target_pairs={{1,0},{2,1},{3,2},{4,3},{5,4},{6,5},{7,6},{8,7},{9,8},{10,9},{11,1... | collective-permute-start | bytes 3293192 | tf_op jit(solution)/shard_map/ppermute | solution.py:282
  3.6 3.1 %collective-permute-start.4 = (f32[67,4096]{1,0:T(8,128)S(1)}, f32[67,4096]{1,0:T(8,128)S(1)}, u32[]{:S(2)}, u32[]{:S(2)}) collective-permute-start(f32[67,4096]{1,0:T(8,128)S(1)} %constant_dynamic-update-slice_fusion._.block), channel_id=1, source_target_pairs={{0,1},{1,2},{2,3},{3,4},{4,5},{5,6},{6,7},{7,8},{8,9},{9,10},{10,1... | collective-permute-start | bytes 3293192 | tf_op jit(solution)/shard_map/ppermute | solution.py:281
  6.8 0.9 %copy-done.2 = f32[8,64,128]{2,1,0:T(8,128)S(1)} copy-done((f32[8,64,128]{2,1,0:T(8,128)S(1)}, f32[8,64,128]{2,1,0:T(8,128)}, u32[]{:S(2)}) %copy-start.2) | copy-done | bytes 262168
  7.7 0.7 copy-done.11
  8.4 1.2 %up.1 = (f32[14,64,128]{2,1,0:T(8,128)S(1)}, s32[6,256]{1,0:T(8,128)S(1)}) custom-call(s32[16,16]{1,0:T(8,128)S(1)} %copy-done.11, f32[64,4096]{1,0:T(8,128)S(1)} %copy-done, f32[16,64,256]{2,1,0:T(8,128)S(1)} %copy-done.1, f32[8,64,128]{2,1,0:T(8,128)S(1)} %copy-done.2, f32[4,64,128]{2,1,0:T(8,128)S(1)} %copy-done.4, ...), custom_call_target="tpu_custom_call" | custom-call | tf_op jit(solution)/shard_map/up/pallas_call | solution.py:297
  9.7 3.0 %collective-permute-start.2 = (f32[14,64,128]{2,1,0:T(8,128)S(1)}, f32[14,64,128]{2,1,0:T(8,128)S(1)}, u32[]{:S(2)}, u32[]{:S(2)}) collective-permute-start(f32[14,64,128]{2,1,0:T(8,128)S(1)} %get-tuple-element.30.refs_0_), channel_id=1, source_target_pairs={{0,2},{1,3},{2,0},{3,1},{4,6},{5,7},{6,4},{7,5},{8,10},{9,11},{10,... | collective-permute-start | bytes 1376264 | tf_op jit(solution)/shard_map/ppermute | solution.py:292
  12.6 3.7 %collective-permute-start.1 = (f32[14,64,128]{2,1,0:T(8,128)S(1)}, f32[14,64,128]{2,1,0:T(8,128)S(1)}, u32[]{:S(2)}, u32[]{:S(2)}) collective-permute-start(f32[14,64,128]{2,1,0:T(8,128)S(1)} %get-tuple-element.30.refs_0_), channel_id=1, source_target_pairs={{0,12},{1,13},{2,14},{3,15},{4,0},{5,1},{6,2},{7,3},{8,4},{9,5},{1... | collective-permute-start | bytes 1376264 | tf_op jit(solution)/shard_map/ppermute | solution.py:292
  16.3 13.4 %near_own.1.refs_0_ = f32[64,4096]{1,0:T(8,128)S(1)} custom-call(s32[6,256]{1,0:T(8,128)S(1)} %get-tuple-element.25.lists, f32[3,4096]{1,0:T(4,128)S(1)} %copy-done.9, f32[67,4096]{1,0:T(8,128)S(1)} %constant_dynamic-update-slice_fusion._.block), custom_call_target="tpu_custom_call" | custom-call | flops 1000000 | bytes 3145728 | tf_op jit(solution)/shard_map/near_own/pallas_call | solution.py:319
  29.7 1.5 %collective-permute-done.2.refs_4_ = f32[14,64,128]{2,1,0:T(8,128)S(1)} collective-permute-done((f32[14,64,128]{2,1,0:T(8,128)S(1)}, f32[14,64,128]{2,1,0:T(8,128)S(1)}, u32[]{:S(2)}, u32[]{:S(2)}) %collective-permute-start.2) | collective-permute-done | bytes 458784 | tf_op jit(solution)/shard_map/ppermute | solution.py:292
  31.2 4.2 %collective-permute-done.1.refs_3_ = f32[14,64,128]{2,1,0:T(8,128)S(1)} collective-permute-done((f32[14,64,128]{2,1,0:T(8,128)S(1)}, f32[14,64,128]{2,1,0:T(8,128)S(1)}, u32[]{:S(2)}, u32[]{:S(2)}) %collective-permute-start.1) | collective-permute-done | bytes 458784 | tf_op jit(solution)/shard_map/ppermute | solution.py:292
  35.4 8.6 %collective-permute-done.refs_2_.refs_1_ = f32[14,64,128]{2,1,0:T(8,128)S(1)} collective-permute-done((f32[14,64,128]{2,1,0:T(8,128)S(1)}, f32[14,64,128]{2,1,0:T(8,128)S(1)}, u32[]{:S(2)}, u32[]{:S(2)}) %collective-permute-start) | collective-permute-done | bytes 458784 | tf_op jit(solution)/shard_map/ppermute | solution.py:292
  44.0 1.5 %collective-permute-start.3 = (f32[14,64,128]{2,1,0:T(8,128)S(1)}, f32[14,64,128]{2,1,0:T(8,128)S(1)}, u32[]{:S(2)}, u32[]{:S(2)}) collective-permute-start(f32[14,64,128]{2,1,0:T(8,128)S(1)} %collective-permute-done.refs_2_.refs_1_), channel_id=1, source_target_pairs={{0,4},{1,5},{2,6},{3,7},{4,8},{5,9},{6,10},{7,11},{8,12},{9,13},{1... | collective-permute-start | bytes 1376264 | tf_op jit(solution)/shard_map/ppermute | solution.py:292
  45.5 1.9 %near_before.1.refs_0_ = f32[64,4096]{1,0:T(8,128)S(1)} custom-call(s32[6,256]{1,0:T(8,128)S(1)} %get-tuple-element.25.lists, f32[3,4096]{1,0:T(4,128)S(1)} %copy-done.9, f32[67,4096]{1,0:T(8,128)S(1)} %collective-permute-done.4.block, f32[64,4096]{1,0:T(8,128)S(1)} %near_own.1.refs_0_, f32[67,4096]{1,0:T(8,128)S(1)} %collective-permute-done.5.refs_1_.block, ...), custom_call_target="tpu_custom_call" | custom-call | flops 10000000000 | bytes 3145728 | tf_op jit(solution)/shard_map/near_before/pallas_call | solution.py:319
  47.5 10.7 %collective-permute-done.3.refs_1_.refs_2_ = f32[14,64,128]{2,1,0:T(8,128)S(1)} collective-permute-done((f32[14,64,128]{2,1,0:T(8,128)S(1)}, f32[14,64,128]{2,1,0:T(8,128)S(1)}, u32[]{:S(2)}, u32[]{:S(2)}) %collective-permute-start.3) | collective-permute-done | bytes 458784 | tf_op jit(solution)/shard_map/ppermute | solution.py:292
  58.7 0.7 collective-permute-start.7
  59.4 1.0 %collective-permute-start.6 = (f32[14,64,128]{2,1,0:T(8,128)S(1)}, f32[14,64,128]{2,1,0:T(8,128)}, u32[]{:S(2)}, u32[]{:S(2)}) collective-permute-start(f32[14,64,128]{2,1,0:T(8,128)S(1)} %collective-permute-done.2.refs_4_), channel_id=1, source_target_pairs={{0,4},{1,5},{2,6},{3,7},{4,8},{5,9},{6,10},{7,11},{8,12},{9,13},{1... | collective-permute-start | bytes 1376264 | tf_op jit(solution)/shard_map/ppermute | solution.py:292
  60.5 10.1 %near_after.1.refs_22_ = f32[64,4096]{1,0:T(8,128)S(1)} custom-call(s32[6,256]{1,0:T(8,128)S(1)} %get-tuple-element.25.lists, f32[3,4096]{1,0:T(4,128)S(1)} %copy-done.9, f32[67,4096]{1,0:T(8,128)S(1)} %collective-permute-done.5.refs_1_.block, f32[64,4096]{1,0:T(8,128)S(1)} %near_before.1.refs_0_, f32[14,64,128]{2,1,0:T(8,128)S(1)} %collective-permute-done.3.refs_1_.refs_2_), custom_call_target="tpu_custom_call" | custom-call | flops 10000000000 | bytes 3145728 | tf_op jit(solution)/shard_map/near_after/pallas_call | solution.py:319
  70.7 1.0 %copy-done.3 = f32[64,4096]{1,0:T(8,128)} copy-done((f32[64,4096]{1,0:T(8,128)}, f32[64,4096]{1,0:T(8,128)S(1)}, u32[]{:S(2)}) %copy-start.3) | copy-done | bytes 1048600
  71.6 1.9 %collective-permute-done.6.refs_5_ = f32[14,64,128]{2,1,0:T(8,128)} collective-permute-done((f32[14,64,128]{2,1,0:T(8,128)S(1)}, f32[14,64,128]{2,1,0:T(8,128)}, u32[]{:S(2)}, u32[]{:S(2)}) %collective-permute-start.6) | collective-permute-done | bytes 458784 | tf_op jit(solution)/shard_map/ppermute | solution.py:292
  74.8 0.8 copy-done.17
  76.9 0.7 collective-permute-done.15.refs_14_
  78.3 11.0 %down.1 = f32[64,4096]{1,0:T(8,128)} custom-call(s32[28,8]{1,0:T(8,128)} %copy-done.10, f32[14,64,128]{2,1,0:T(8,128)} %copy-done.5, f32[14,64,128]{2,1,0:T(8,128)} %copy-done.7, f32[14,64,128]{2,1,0:T(8,128)} %copy-done.8, f32[14,64,128]{2,1,0:T(8,128)} %copy-done.6, f32[14,64,128]{2,1,0:T(8,128)} %copy-done.14, ...), custom_call_target="tpu_custom_call" | custom-call | tf_op jit(solution)/shard_map/down/pallas_call | solution.py:381
  (63 shorter events, 4.0 us)
Async XLA Ops:
  2.3 43.2 %collective-permute-start.5 = (f32[67,4096]{1,0:T(8,128)S(1)}, f32[67,4096]{1,0:T(8,128)S(1)}, u32[]{:S(2)}, u32[]{:S(2)}) collective-permute-start(f32[67,4096]{1,0:T(8,128)S(1)} %constant_dynamic-update-slice_fusion._.block), channel_id=1, source_target_pairs={{1,0},{2,1},{3,2},{4,3},{5,4},{6,5},{7,6},{8,7},{9,8},{10,9},{11,1... | collective-permute-start | bytes 3293192 | tf_op jit(solution)/shard_map/ppermute | solution.py:282
  3.6 41.9 %collective-permute-start.4 = (f32[67,4096]{1,0:T(8,128)S(1)}, f32[67,4096]{1,0:T(8,128)S(1)}, u32[]{:S(2)}, u32[]{:S(2)}) collective-permute-start(f32[67,4096]{1,0:T(8,128)S(1)} %constant_dynamic-update-slice_fusion._.block), channel_id=1, source_target_pairs={{0,1},{1,2},{2,3},{3,4},{4,5},{5,6},{6,7},{7,8},{8,9},{9,10},{10,1... | collective-permute-start | bytes 3293192 | tf_op jit(solution)/shard_map/ppermute | solution.py:281
  9.7 48.5 %copy-start.5 = (f32[14,64,128]{2,1,0:T(8,128)}, f32[14,64,128]{2,1,0:T(8,128)S(1)}, u32[]{:S(2)}) copy-start(f32[14,64,128]{2,1,0:T(8,128)S(1)} %get-tuple-element.30.refs_0_) | copy-start | bytes 1376260
  9.7 21.5 %collective-permute-start.2 = (f32[14,64,128]{2,1,0:T(8,128)S(1)}, f32[14,64,128]{2,1,0:T(8,128)S(1)}, u32[]{:S(2)}, u32[]{:S(2)}) collective-permute-start(f32[14,64,128]{2,1,0:T(8,128)S(1)} %get-tuple-element.30.refs_0_), channel_id=1, source_target_pairs={{0,2},{1,3},{2,0},{3,1},{4,6},{5,7},{6,4},{7,5},{8,10},{9,11},{10,... | collective-permute-start | bytes 1376264 | tf_op jit(solution)/shard_map/ppermute | solution.py:292
  12.6 22.8 %collective-permute-start.1 = (f32[14,64,128]{2,1,0:T(8,128)S(1)}, f32[14,64,128]{2,1,0:T(8,128)S(1)}, u32[]{:S(2)}, u32[]{:S(2)}) collective-permute-start(f32[14,64,128]{2,1,0:T(8,128)S(1)} %get-tuple-element.30.refs_0_), channel_id=1, source_target_pairs={{0,12},{1,13},{2,14},{3,15},{4,0},{5,1},{6,2},{7,3},{8,4},{9,5},{1... | collective-permute-start | bytes 1376264 | tf_op jit(solution)/shard_map/ppermute | solution.py:292
  16.3 27.7 %collective-permute-start = (f32[14,64,128]{2,1,0:T(8,128)S(1)}, f32[14,64,128]{2,1,0:T(8,128)S(1)}, u32[]{:S(2)}, u32[]{:S(2)}) collective-permute-start(f32[14,64,128]{2,1,0:T(8,128)S(1)} %get-tuple-element.30.refs_0_), channel_id=1, source_target_pairs={{0,4},{1,5},{2,6},{3,7},{4,8},{5,9},{6,10},{7,11},{8,12},{9,13},{1... | collective-permute-start | bytes 1376264 | tf_op jit(solution)/shard_map/ppermute | solution.py:292
  31.2 29.2 %copy-start.14 = (f32[14,64,128]{2,1,0:T(8,128)}, f32[14,64,128]{2,1,0:T(8,128)S(1)}, u32[]{:S(2)}) copy-start(f32[14,64,128]{2,1,0:T(8,128)S(1)} %collective-permute-done.2.refs_4_) | copy-start | bytes 1376260
  35.4 38.1 %copy-start.6 = (f32[14,64,128]{2,1,0:T(8,128)}, f32[14,64,128]{2,1,0:T(8,128)S(1)}, u32[]{:S(2)}) copy-start(f32[14,64,128]{2,1,0:T(8,128)S(1)} %collective-permute-done.1.refs_3_) | copy-start | bytes 1376260
  44.0 14.1 %collective-permute-start.3 = (f32[14,64,128]{2,1,0:T(8,128)S(1)}, f32[14,64,128]{2,1,0:T(8,128)S(1)}, u32[]{:S(2)}, u32[]{:S(2)}) collective-permute-start(f32[14,64,128]{2,1,0:T(8,128)S(1)} %collective-permute-done.refs_2_.refs_1_), channel_id=1, source_target_pairs={{0,4},{1,5},{2,6},{3,7},{4,8},{5,9},{6,10},{7,11},{8,12},{9,13},{1... | collective-permute-start | bytes 1376264 | tf_op jit(solution)/shard_map/ppermute | solution.py:292
  45.5 14.9 %collective-permute-start.8 = (f32[14,64,128]{2,1,0:T(8,128)S(1)}, f32[14,64,128]{2,1,0:T(8,128)S(1)}, u32[]{:S(2)}, u32[]{:S(2)}) collective-permute-start(f32[14,64,128]{2,1,0:T(8,128)S(1)} %collective-permute-done.1.refs_3_), channel_id=1, source_target_pairs={{0,2},{1,3},{2,0},{3,1},{4,6},{5,7},{6,4},{7,5},{8,10},{9,11},{10,... | collective-permute-start | bytes 1376264 | tf_op jit(solution)/shard_map/ppermute | solution.py:292
  47.4 28.3 %copy-start.21 = (s32[16,8]{0,1:T(8,128)S(1)}, s32[16,8]{0,1:T(8,128)}, u32[]{:S(2)}) copy-start(s32[16,8]{0,1:T(8,128)} %param.21) | copy-start | bytes 1540
  47.4 28.3 %copy-start.12 = (s32[8,8]{1,0:T(8,128)S(1)}, s32[8,8]{1,0:T(8,128)}, u32[]{:S(2)}) copy-start(s32[8,8]{1,0:T(8,128)} %far_one.1) | copy-start | bytes 772
  47.4 28.3 %copy-start.13 = (s32[4,8]{1,0:T(4,128)S(1)}, s32[4,8]{1,0:T(4,128)}, u32[]{:S(2)}) copy-start(s32[4,8]{1,0:T(4,128)} %far_two.1) | copy-start | bytes 388
  58.1 15.4 %copy-start.8 = (f32[14,64,128]{2,1,0:T(8,128)}, f32[14,64,128]{2,1,0:T(8,128)S(1)}, u32[]{:S(2)}) copy-start(f32[14,64,128]{2,1,0:T(8,128)S(1)} %collective-permute-done.3.refs_1_.refs_2_) | copy-start | bytes 1376260
  58.1 16.0 %collective-permute-start.9 = (f32[14,64,128]{2,1,0:T(8,128)S(1)}, f32[14,64,128]{2,1,0:T(8,128)S(1)}, u32[]{:S(2)}, u32[]{:S(2)}) collective-permute-start(f32[14,64,128]{2,1,0:T(8,128)S(1)} %get-tuple-element.30.refs_0_), channel_id=1, source_target_pairs={{0,1},{1,0},{2,3},{3,2},{4,5},{5,4},{6,7},{7,6},{8,9},{9,8},{10,11... | collective-permute-start | bytes 1376264 | tf_op jit(solution)/shard_map/ppermute | solution.py:292
  58.2 16.4 %collective-permute-start.10 = (f32[14,64,128]{2,1,0:T(8,128)S(1)}, f32[14,64,128]{2,1,0:T(8,128)S(1)}, u32[]{:S(2)}, u32[]{:S(2)}) collective-permute-start(f32[14,64,128]{2,1,0:T(8,128)S(1)} %collective-permute-done.refs_2_.refs_1_), channel_id=1, source_target_pairs={{0,1},{1,0},{2,3},{3,2},{4,5},{5,4},{6,7},{7,6},{8,9},{9,8},{10,11... | collective-permute-start | bytes 1376264 | tf_op jit(solution)/shard_map/ppermute | solution.py:292
  58.7 14.9 %collective-permute-start.7 = (f32[14,64,128]{2,1,0:T(8,128)S(1)}, f32[14,64,128]{2,1,0:T(8,128)}, u32[]{:S(2)}, u32[]{:S(2)}) collective-permute-start(f32[14,64,128]{2,1,0:T(8,128)S(1)} %collective-permute-done.3.refs_1_.refs_2_), channel_id=1, source_target_pairs={{0,2},{1,3},{2,0},{3,1},{4,6},{5,7},{6,4},{7,5},{8,10},{9,11},{10,... | collective-permute-start | bytes 1376264 | tf_op jit(solution)/shard_map/ppermute | solution.py:292
  59.4 14.1 %collective-permute-start.6 = (f32[14,64,128]{2,1,0:T(8,128)S(1)}, f32[14,64,128]{2,1,0:T(8,128)}, u32[]{:S(2)}, u32[]{:S(2)}) collective-permute-start(f32[14,64,128]{2,1,0:T(8,128)S(1)} %collective-permute-done.2.refs_4_), channel_id=1, source_target_pairs={{0,4},{1,5},{2,6},{3,7},{4,8},{5,9},{6,10},{7,11},{8,12},{9,13},{1... | collective-permute-start | bytes 1376264 | tf_op jit(solution)/shard_map/ppermute | solution.py:292
  60.4 13.6 %collective-permute-start.13 = (f32[14,64,128]{2,1,0:T(8,128)S(1)}, f32[14,64,128]{2,1,0:T(8,128)S(1)}, u32[]{:S(2)}, u32[]{:S(2)}) collective-permute-start(f32[14,64,128]{2,1,0:T(8,128)S(1)} %collective-permute-done.2.refs_4_), channel_id=1, source_target_pairs={{0,1},{1,0},{2,3},{3,2},{4,5},{5,4},{6,7},{7,6},{8,9},{9,8},{10,11... | collective-permute-start | bytes 1376264 | tf_op jit(solution)/shard_map/ppermute | solution.py:292
  73.5 2.9 %collective-permute-start.12 = (f32[14,64,128]{2,1,0:T(8,128)S(1)}, f32[14,64,128]{2,1,0:T(8,128)}, u32[]{:S(2)}, u32[]{:S(2)}) collective-permute-start(f32[14,64,128]{2,1,0:T(8,128)S(1)} %collective-permute-done.1.refs_3_), channel_id=1, source_target_pairs={{0,1},{1,0},{2,3},{3,2},{4,5},{5,4},{6,7},{7,6},{8,9},{9,8},{10,11... | collective-permute-start | bytes 1376264 | tf_op jit(solution)/shard_map/ppermute | solution.py:292
  73.5 3.2 %collective-permute-start.11 = (f32[14,64,128]{2,1,0:T(8,128)S(1)}, f32[14,64,128]{2,1,0:T(8,128)}, u32[]{:S(2)}, u32[]{:S(2)}) collective-permute-start(f32[14,64,128]{2,1,0:T(8,128)S(1)} %collective-permute-done.3.refs_1_.refs_2_), channel_id=1, source_target_pairs={{0,1},{1,0},{2,3},{3,2},{4,5},{5,4},{6,7},{7,6},{8,9},{9,8},{10,11... | collective-permute-start | bytes 1376264 | tf_op jit(solution)/shard_map/ppermute | solution.py:292
  74.1 2.8 %collective-permute-start.14 = (f32[14,64,128]{2,1,0:T(8,128)}, f32[14,64,128]{2,1,0:T(8,128)S(1)}, u32[]{:S(2)}, u32[]{:S(2)}) collective-permute-start(f32[14,64,128]{2,1,0:T(8,128)} %collective-permute-done.6.refs_5_), channel_id=1, source_target_pairs={{0,1},{1,0},{2,3},{3,2},{4,5},{5,4},{6,7},{7,6},{8,9},{9,8},{10,11... | collective-permute-start | bytes 1376264 | tf_op jit(solution)/shard_map/ppermute | solution.py:292
  74.1 3.4 %collective-permute-start.15 = (f32[14,64,128]{2,1,0:T(8,128)}, f32[14,64,128]{2,1,0:T(8,128)S(1)}, u32[]{:S(2)}, u32[]{:S(2)}) collective-permute-start(f32[14,64,128]{2,1,0:T(8,128)} %collective-permute-done.7.refs_6_), channel_id=1, source_target_pairs={{0,1},{1,0},{2,3},{3,2},{4,5},{5,4},{6,7},{7,6},{8,9},{9,8},{10,11... | collective-permute-start | bytes 1376264 | tf_op jit(solution)/shard_map/ppermute | solution.py:292
  75.6 2.5 %collective-permute-start.16 = (f32[14,64,128]{2,1,0:T(8,128)S(1)}, f32[14,64,128]{2,1,0:T(8,128)}, u32[]{:S(2)}, u32[]{:S(2)}) collective-permute-start(f32[14,64,128]{2,1,0:T(8,128)S(1)} %collective-permute-done.8.refs_7_), channel_id=1, source_target_pairs={{0,1},{1,0},{2,3},{3,2},{4,5},{5,4},{6,7},{7,6},{8,9},{9,8},{10,11... | collective-permute-start | bytes 1376264 | tf_op jit(solution)/shard_map/ppermute | solution.py:292
  (15 other events, 67.3 us)

commit v3 on v2

--- a/solution.py
+++ b/solution.py
@@ -17,6 +17,7 @@
 GROUP = 8
 NEAR_WORK = 10**10
 OWN_WORK = 10**6
+NEAR_MEBIBYTES = 16
 DOWN_MEBIBYTES = 56
 
 
@@ -27,34 +28,46 @@
 
 
 def product(left, right, dims):
-    left_high, left_low = halves(left)
-    right_high, right_low = halves(right)
-    dot = functools.partial(lax.dot_general, preferred_element_type=jnp.float32)
-    return (
-        dot(left_high, right_high, dims)
-        + dot(left_high, right_low, dims)
-        + dot(left_low, right_high, dims)
+    across = 1 if dims == NN else 0
+    both = lax.dot_general(
+        jnp.concatenate(halves(left), axis=0),
+        jnp.concatenate(halves(right), axis=across),
+        dims,
+        preferred_element_type=jnp.float32,
     )
+    rows = left.shape[0]
+    return both[:rows] + both[rows:]
+
+
+def folded(wide):
+    return wide + pltpu.roll(wide, wide.shape[1] // 2, 1)
+
+
+def narrow(wide):
+    width = wide.shape[1] // 2
+    return wide[:, :width] + wide[:, width:]
+
+
+def pair_of(even, odd):
+    lane = lax.broadcasted_iota(jnp.int32, even.shape, 1)
+    return jnp.where(lane < even.shape[1] // 2, folded(even), folded(odd))
 
 
 def up_kernel(neighbours, vectors, basis, first, second, _, out, lists):
     me = lax.axis_index("leaf")
     leaves, _, size = basis.shape
-    rank = basis.shape[1]
     pairs = []
     for pair in range(leaves // 2):
         both = []
         for leaf in (2 * pair, 2 * pair + 1):
             columns = vectors[:, leaf * size : (leaf + 1) * size]
             both.append(product(columns, basis[leaf], NT))
-        pairs.append(jnp.concatenate(both, axis=1))
+        pairs.append(pair_of(*both))
         out[pair] = pairs[pair]
     base = len(pairs)
     for transfer in (first, second):
         nodes = [product(pairs[i], transfer[i], NT) for i in range(len(pairs))]
-        pairs = [
-            jnp.concatenate(nodes[2 * i : 2 * i + 2], axis=1) for i in range(len(nodes) // 2)
-        ]
+        pairs = [pair_of(*nodes[2 * i : 2 * i + 2]) for i in range(len(nodes) // 2)]
         for i, pair in enumerate(pairs):
             out[base + i] = pair
         base += len(pairs)
@@ -142,7 +155,19 @@
         out[i + 3 : i + 4] = jnp.broadcast_to(total, (1, width)).astype(jnp.int32)
 
 
-def near_kernel(which, leaves, lists, p_own, block, *refs):
+def pack_kernel(vectors, points, out, sem):
+    width = vectors.shape[1]
+    copy = pltpu.make_async_copy(vectors, out.at[:, pl.ds(0, width)], sem)
+    copy.start()
+    size = out.shape[1] - width
+    out[:, width:] = jnp.zeros((out.shape[0], size), jnp.float32)
+    for leaf in range(width // size):
+        cut = slice(leaf * size, (leaf + 1) * size)
+        out[4 * leaf : 4 * leaf + 3, width:] = points[:, cut]
+    copy.wait()
+
+
+def near_kernel(which, part, leaves, lists, p_own, block, *refs):
     so_far = None if which == 1 else refs[0]
     out, split, source, target, total = refs[-5:]
     rhs, size = split.shape[1] // 2, split.shape[2]
@@ -151,7 +176,8 @@
     bottom = jnp.min(own, axis=1, keepdims=True)
     centre = 0.5 * (top + bottom)
     wide = features(own, centre, False).astype(jnp.bfloat16)
-    there = features(block[rhs : rhs + 3], centre, True)
+    wide_points = [block[4 * leaf : 4 * leaf + 3, leaves * size :] for leaf in range(leaves)]
+    there = features(jnp.concatenate(wide_points, axis=1), centre, True)
     for leaf in range(leaves):
         cut = slice(leaf * size, (leaf + 1) * size)
         target[leaf] = wide[:, cut]
@@ -177,7 +203,10 @@
             total[into] += (dot(both, high, NN) + dot(both, low, NN)) * times
         return carry
 
-    lax.fori_loop(0, (lists[which + 3, 0] + GROUP - 1) // GROUP, group, 0)
+    groups = (lists[which + 3, 0] + GROUP - 1) // GROUP
+    numerator, parts = part
+    start, stop = groups * numerator // parts, groups * (numerator + 1) // parts
+    lax.fori_loop(start, stop, group, 0)
     for leaf in range(leaves):
         cut = slice(leaf * size, (leaf + 1) * size)
         value = (total[leaf, :rhs] + total[leaf, rhs:]) * LN2
@@ -215,15 +244,17 @@
         return product(jnp.concatenate(pieces, axis=1), coupling, NT)
 
     def level(base, coupling):
+        width = min(4, coupling.shape[0] // 2)
+
         def step(i, carry):
-            for j in range(2):
-                at = 2 * i + j
+            for j in range(width):
+                at = width * i + j
                 even = field(2 * (base + at), coupling[2 * at])
                 odd = field(2 * (base + at) + 1, coupling[2 * at + 1])
-                fields[base + at] = jnp.concatenate([even, odd], axis=1)
+                fields[base + at] = pair_of(even, odd)
             return carry
 
-        lax.fori_loop(0, coupling.shape[0] // 4, step, 0)
+        lax.fori_loop(0, coupling.shape[0] // (2 * width), step, 0)
 
     level(leaves // 2 + leaves // 4, c_two)
     copies[len(slots) + 2].wait()
@@ -237,16 +268,16 @@
     for p in range(leaves // 4):
         pair = fields[leaves // 2 + leaves // 4 + p // 2]
         top = pair[:, :rank] if p % 2 == 0 else pair[:, rank:]
-        ones.append(fields[leaves // 2 + p] + product(top, second[p], NN))
+        ones.append(fields[leaves // 2 + p] + narrow(product(top, second[p], NN)))
     for p in range(leaves // 2):
         pair = ones[p // 2]
         top = pair[:, :rank] if p % 2 == 0 else pair[:, rank:]
-        zeros = fields[p] + product(top, first[p], NN)
+        zeros = fields[p] + narrow(product(top, first[p], NN))
         for half in range(2):
             leaf = 2 * p + half
             low = zeros[:, :rank] if half == 0 else zeros[:, rank:]
             cut = slice(leaf * size, (leaf + 1) * size)
-            out[:, cut] += product(low, basis[leaf], NN)
+            out[:, cut] += narrow(product(low, basis[leaf], NN))
 
 
 def whole_vmem(n):
@@ -277,7 +308,15 @@
     tie = lax.optimization_barrier
     before = [(i, i + 1) for i in range(devices - 1)]
     after = [(i + 1, i) for i in range(devices - 1)]
-    stacked = jnp.concatenate([input_vectors, points], axis=0)
+    stacked = pl.pallas_call(
+        pack_kernel,
+        out_shape=jax.ShapeDtypeStruct((rhs, points.shape[1] + size), jnp.float32),
+        in_specs=[pl.BlockSpec(memory_space=pl.ANY), pl.BlockSpec(memory_space=pltpu.VMEM)],
+        out_specs=pl.BlockSpec(memory_space=pltpu.VMEM),
+        scratch_shapes=[pltpu.SemaphoreType.DMA(())],
+        compiler_params=params(8),
+        name="pack",
+    )(input_vectors, points)
     from_before = lax.ppermute(stacked, "leaf", before)
     from_after = lax.ppermute(stacked, "leaf", after)
 
@@ -314,10 +353,10 @@
         name="picks",
     )(far_zero, far_one, far_two)
 
-    def near_field(which, operand, work, near, *later):
-        operands = (operand,) if near is None else (operand, near)
+    def near_field(which, part, block, work, near, *later):
+        operands = (block,) if near is None else (block, near)
         return pl.pallas_call(
-            functools.partial(near_kernel, which, leaves),
+            functools.partial(near_kernel, which, part, leaves),
             out_shape=jax.ShapeDtypeStruct(input_vectors.shape, jnp.float32),
             in_specs=[pl.BlockSpec(memory_space=pltpu.SMEM)]
             + whole_vmem(1 + len(operands))
@@ -332,7 +371,7 @@
             cost_estimate=pl.CostEstimate(
                 flops=work, bytes_accessed=3 * 2**20, transcendentals=0
             ),
-            compiler_params=params(16),
+            compiler_params=params(NEAR_MEBIBYTES),
             name=("near_before", "near_own", "near_after")[which],
         )(lists, points, *operands, *later)
 
@@ -341,7 +380,7 @@
     for step, towards in {1: 1, far_end: -1}.items():
         held[0, step] = swap(coeffs, towards, 0, 0)
     held[1, 0] = swap(coeffs, 0, 1, 0)
-    near = near_field(1, stacked, OWN_WORK, None)
+    near = near_field(1, (0, 1), stacked, OWN_WORK, None)
     held, near = tie((held, near))
     middle = (lines + 1) // 2
     for step in range(2, middle + 1):
@@ -352,17 +391,17 @@
     if far_end > 1:
         held[1, far_end] = swap(held[0, far_end], 0, 1, 0)
     ends = [held[0, step] for step in sorted({1, far_end})]
-    near = near_field(0, from_before, NEAR_WORK, near, from_after, *ends)
+    near = near_field(0, (0, 1), from_before, NEAR_WORK, near, from_after, *ends)
     along, near = tie(([held[0, step] for step in range(lines)], near))
+    for step in range(2, far_end):
+        held[1, step] = swap(along[step], 0, 1, 0)
     if (1, 1) not in held:
         behind, _ = tie((held[1, 0], along))
         held[1, 1] = swap(behind, 1, 0, 0)
-    for step in range(2, far_end):
-        held[1, step] = swap(along[step], 0, 1, 0)
     early = {(0, step): value for step, value in enumerate(along)}
     early[1, 0], near = tie((held[1, 0], near))
     across = {key: swap(value, 0, 0, 1) for key, value in early.items()}
-    near = near_field(2, from_after, NEAR_WORK, near, *along[2:far_end])
+    near = near_field(2, (0, 1), from_after, NEAR_WORK, near, *along[2:far_end])
     late = {key: value for key, value in held.items() if key not in early}
     late, near = tie((late, near))
     across.update({key: swap(value, 0, 0, 1) for key, value in late.items()})

time: 89.7 us -> 88.2 us (0.983)
  starting transfers between devices: 15.9 us -> 14.8 us
    ppermute x15, starting transfers between devices: 11.5 us -> 10.2 us  [swap(): return lax.ppermute(value, 'leaf', pairs)]
    unnamed x46 -> x49, local copies, waits for them, and re-layouts: 6.06 us -> 6.67 us
    pallas_call x3 -> x4, Pallas kernels: 25.4 us -> 25.6 us  [the longest x3 25.5 us: near_field(): pl.pallas_call(functools.partial(near_kernel, which, part, leaves), out_s...]
where the time goes in v3:
time: 88.2 us; the launch traced here: 87.9 us
  Pallas kernels  37.6 us (43%)
  waiting for transfers between devices  28.5 us (32%)
  starting transfers between devices  14.8 us (17%)
  local copies, waits for them, and re-layouts  6.67 us (8%)
    ppermute x15, waiting for transfers between devices, swap(): return lax.ppermute(value, 'leaf', pairs)  28.5 us
    pallas_call x3, Pallas kernels, near_field(): pl.pallas_call(functools.partial(near_kernel, which, part, leaves), out_s...  25.5 us
    pallas_call x1, Pallas kernels, on_device(): pl.pallas_call(down_kernel, out_shape=jax.ShapeDtypeStruct(input_vectors....  10.8 us
    ppermute x15, starting transfers between devices, swap(): return lax.ppermute(value, 'leaf', pairs)  10.2 us
    unnamed x49, local copies, waits for them, and re-layouts  6.67 us
    ppermute x1, starting transfers between devices, on_device(): from_before = lax.ppermute(stacked, 'leaf', before)  3.1 us
  transfers between devices with their start and end apart: 17, of which 9 were waited for; matrix products, arithmetic and copies ran while one was open for 0% of the time, Pallas kernels for 30%

profile of v3, /device:TPU:0, one launch (start us, length us, event | category | flops | bytes accessed | tf_op | source)
XLA Modules:
  0.0 87.9 jit_solution(4796180511879468890)
XLA Ops:
  0.0 1.2 %copy-done = f32[64,4096]{1,0:T(8,128)S(1)} copy-done((f32[64,4096]{1,0:T(8,128)S(1)}, f32[64,4096]{1,0:T(8,128)}, u32[]{:S(2)}) %copy-start) | copy-done | bytes 1048600
  1.2 0.8 copy-done.10
  2.2 1.4 %collective-permute-start.5 = (f32[64,4352]{1,0:T(8,128)S(1)}, f32[64,4352]{1,0:T(8,128)S(1)}, u32[]{:S(2)}, u32[]{:S(2)}) collective-permute-start(f32[64,4352]{1,0:T(8,128)S(1)} %pack.1._.block), channel_id=1, source_target_pairs={{1,0},{2,1},{3,2},{4,3},{5,4},{6,5},{7,6},{8,7},{9,8},{10,9},{11,1... | collective-permute-start | bytes 3342344 | tf_op jit(solution)/shard_map/ppermute | solution.py:321
  3.6 3.1 %collective-permute-start.4 = (f32[64,4352]{1,0:T(8,128)S(1)}, f32[64,4352]{1,0:T(8,128)S(1)}, u32[]{:S(2)}, u32[]{:S(2)}) collective-permute-start(f32[64,4352]{1,0:T(8,128)S(1)} %pack.1._.block), channel_id=1, source_target_pairs={{0,1},{1,2},{2,3},{3,4},{4,5},{5,6},{6,7},{7,8},{8,9},{9,10},{10,1... | collective-permute-start | bytes 3342344 | tf_op jit(solution)/shard_map/ppermute | solution.py:320
  6.8 0.9 %copy-done.3 = f32[8,64,128]{2,1,0:T(8,128)S(1)} copy-done((f32[8,64,128]{2,1,0:T(8,128)S(1)}, f32[8,64,128]{2,1,0:T(8,128)}, u32[]{:S(2)}) %copy-start.3) | copy-done | bytes 262168
  7.7 0.7 copy-done.13
  8.4 1.1 %up.1 = (f32[14,64,128]{2,1,0:T(8,128)S(1)}, s32[6,256]{1,0:T(8,128)S(1)}) custom-call(s32[16,16]{1,0:T(8,128)S(1)} %copy-done.13, f32[64,4096]{1,0:T(8,128)S(1)} %copy-done.1, f32[16,64,256]{2,1,0:T(8,128)S(1)} %copy-done.2, f32[8,64,128]{2,1,0:T(8,128)S(1)} %copy-done.3, f32[4,64,128]{2,1,0:T(8,128)S(1)} %copy-done.5, f32[64,4352]{1,0:T(8,128)S(1)} %pack.1._.block), custom_call_target="tpu_custom_call" | custom-call | tf_op jit(solution)/shard_map/up/pallas_call | solution.py:336
  9.5 3.0 %collective-permute-start.2 = (f32[14,64,128]{2,1,0:T(8,128)S(1)}, f32[14,64,128]{2,1,0:T(8,128)S(1)}, u32[]{:S(2)}, u32[]{:S(2)}) collective-permute-start(f32[14,64,128]{2,1,0:T(8,128)S(1)} %get-tuple-element.30.refs_0_), channel_id=1, source_target_pairs={{0,2},{1,3},{2,0},{3,1},{4,6},{5,7},{6,4},{7,5},{8,10},{9,11},{10,... | collective-permute-start | bytes 1376264 | tf_op jit(solution)/shard_map/ppermute | solution.py:331
  12.5 3.7 %collective-permute-start.1 = (f32[14,64,128]{2,1,0:T(8,128)S(1)}, f32[14,64,128]{2,1,0:T(8,128)S(1)}, u32[]{:S(2)}, u32[]{:S(2)}) collective-permute-start(f32[14,64,128]{2,1,0:T(8,128)S(1)} %get-tuple-element.30.refs_0_), channel_id=1, source_target_pairs={{0,12},{1,13},{2,14},{3,15},{4,0},{5,1},{6,2},{7,3},{8,4},{9,5},{1... | collective-permute-start | bytes 1376264 | tf_op jit(solution)/shard_map/ppermute | solution.py:331
  16.1 13.4 %near_own.1.refs_0_ = f32[64,4096]{1,0:T(8,128)S(1)} custom-call(s32[6,256]{1,0:T(8,128)S(1)} %get-tuple-element.25.lists, f32[3,4096]{1,0:T(4,128)S(1)} %copy-done.11, f32[64,4352]{1,0:T(8,128)S(1)} %pack.1._.block), custom_call_target="tpu_custom_call" | custom-call | flops 1000000 | bytes 3145728 | tf_op jit(solution)/shard_map/near_own/pallas_call | solution.py:358
  29.6 0.9 %collective-permute-done.2.refs_4_ = f32[14,64,128]{2,1,0:T(8,128)S(1)} collective-permute-done((f32[14,64,128]{2,1,0:T(8,128)S(1)}, f32[14,64,128]{2,1,0:T(8,128)S(1)}, u32[]{:S(2)}, u32[]{:S(2)}) %collective-permute-start.2) | collective-permute-done | bytes 458784 | tf_op jit(solution)/shard_map/ppermute | solution.py:331
  30.5 3.7 %collective-permute-done.1.refs_3_ = f32[14,64,128]{2,1,0:T(8,128)S(1)} collective-permute-done((f32[14,64,128]{2,1,0:T(8,128)S(1)}, f32[14,64,128]{2,1,0:T(8,128)S(1)}, u32[]{:S(2)}, u32[]{:S(2)}) %collective-permute-start.1) | collective-permute-done | bytes 458784 | tf_op jit(solution)/shard_map/ppermute | solution.py:331
  34.2 9.1 %collective-permute-done.refs_2_.refs_1_ = f32[14,64,128]{2,1,0:T(8,128)S(1)} collective-permute-done((f32[14,64,128]{2,1,0:T(8,128)S(1)}, f32[14,64,128]{2,1,0:T(8,128)S(1)}, u32[]{:S(2)}, u32[]{:S(2)}) %collective-permute-start) | collective-permute-done | bytes 458784 | tf_op jit(solution)/shard_map/ppermute | solution.py:331
  43.3 0.8 collective-permute-start.3
  44.1 1.9 %near_before.1.refs_0_ = f32[64,4096]{1,0:T(8,128)S(1)} custom-call(s32[6,256]{1,0:T(8,128)S(1)} %get-tuple-element.25.lists, f32[3,4096]{1,0:T(4,128)S(1)} %copy-done.11, f32[64,4352]{1,0:T(8,128)S(1)} %collective-permute-done.4.block, f32[64,4096]{1,0:T(8,128)S(1)} %near_own.1.refs_0_, f32[64,4352]{1,0:T(8,128)S(1)} %collective-permute-done.5.refs_1_.block, ...), custom_call_target="tpu_custom_call" | custom-call | flops 10000000000 | bytes 3145728 | tf_op jit(solution)/shard_map/near_before/pallas_call | solution.py:358
  46.0 10.7 %collective-permute-done.3.refs_1_.refs_2_ = f32[14,64,128]{2,1,0:T(8,128)S(1)} collective-permute-done((f32[14,64,128]{2,1,0:T(8,128)S(1)}, f32[14,64,128]{2,1,0:T(8,128)S(1)}, u32[]{:S(2)}, u32[]{:S(2)}) %collective-permute-start.3) | collective-permute-done | bytes 458784 | tf_op jit(solution)/shard_map/ppermute | solution.py:331
  57.2 0.7 collective-permute-start.7
  58.4 10.2 %near_after.1.refs_22_ = f32[64,4096]{1,0:T(8,128)S(1)} custom-call(s32[6,256]{1,0:T(8,128)S(1)} %get-tuple-element.25.lists, f32[3,4096]{1,0:T(4,128)S(1)} %copy-done.11, f32[64,4352]{1,0:T(8,128)S(1)} %collective-permute-done.5.refs_1_.block, f32[64,4096]{1,0:T(8,128)S(1)} %near_before.1.refs_0_, f32[14,64,128]{2,1,0:T(8,128)S(1)} %collective-permute-done.3.refs_1_.refs_2_), custom_call_target="tpu_custom_call" | custom-call | flops 10000000000 | bytes 3145728 | tf_op jit(solution)/shard_map/near_after/pallas_call | solution.py:358
  68.7 1.0 %copy-done.4 = f32[64,4096]{1,0:T(8,128)} copy-done((f32[64,4096]{1,0:T(8,128)}, f32[64,4096]{1,0:T(8,128)S(1)}, u32[]{:S(2)}) %copy-start.4) | copy-done | bytes 1048600
  69.7 2.4 %collective-permute-done.6.refs_5_ = f32[14,64,128]{2,1,0:T(8,128)} collective-permute-done((f32[14,64,128]{2,1,0:T(8,128)S(1)}, f32[14,64,128]{2,1,0:T(8,128)}, u32[]{:S(2)}, u32[]{:S(2)}) %collective-permute-start.6) | collective-permute-done | bytes 458784 | tf_op jit(solution)/shard_map/ppermute | solution.py:331
  73.4 0.8 copy-done.19
  74.4 0.6 copy-done.12
  75.4 0.7 collective-permute-done.15.refs_14_
  76.9 10.8 %down.1 = f32[64,4096]{1,0:T(8,128)} custom-call(s32[28,8]{1,0:T(8,128)} %copy-done.12, f32[14,64,128]{2,1,0:T(8,128)} %copy-done.6, f32[14,64,128]{2,1,0:T(8,128)} %copy-done.8, f32[14,64,128]{2,1,0:T(8,128)} %copy-done.9, f32[14,64,128]{2,1,0:T(8,128)} %copy-done.7, f32[14,64,128]{2,1,0:T(8,128)} %copy-done.16, ...), custom_call_target="tpu_custom_call" | custom-call | tf_op jit(solution)/shard_map/down/pallas_call | solution.py:420
  (66 shorter events, 3.9 us)
Async XLA Ops:
  2.2 41.9 %collective-permute-start.5 = (f32[64,4352]{1,0:T(8,128)S(1)}, f32[64,4352]{1,0:T(8,128)S(1)}, u32[]{:S(2)}, u32[]{:S(2)}) collective-permute-start(f32[64,4352]{1,0:T(8,128)S(1)} %pack.1._.block), channel_id=1, source_target_pairs={{1,0},{2,1},{3,2},{4,3},{5,4},{6,5},{7,6},{8,7},{9,8},{10,9},{11,1... | collective-permute-start | bytes 3342344 | tf_op jit(solution)/shard_map/ppermute | solution.py:321
  3.6 40.5 %collective-permute-start.4 = (f32[64,4352]{1,0:T(8,128)S(1)}, f32[64,4352]{1,0:T(8,128)S(1)}, u32[]{:S(2)}, u32[]{:S(2)}) collective-permute-start(f32[64,4352]{1,0:T(8,128)S(1)} %pack.1._.block), channel_id=1, source_target_pairs={{0,1},{1,2},{2,3},{3,4},{4,5},{5,6},{6,7},{7,8},{8,9},{9,10},{10,1... | collective-permute-start | bytes 3342344 | tf_op jit(solution)/shard_map/ppermute | solution.py:320
  9.5 47.2 %copy-start.6 = (f32[14,64,128]{2,1,0:T(8,128)}, f32[14,64,128]{2,1,0:T(8,128)S(1)}, u32[]{:S(2)}) copy-start(f32[14,64,128]{2,1,0:T(8,128)S(1)} %get-tuple-element.30.refs_0_) | copy-start | bytes 1376260
  9.5 21.0 %collective-permute-start.2 = (f32[14,64,128]{2,1,0:T(8,128)S(1)}, f32[14,64,128]{2,1,0:T(8,128)S(1)}, u32[]{:S(2)}, u32[]{:S(2)}) collective-permute-start(f32[14,64,128]{2,1,0:T(8,128)S(1)} %get-tuple-element.30.refs_0_), channel_id=1, source_target_pairs={{0,2},{1,3},{2,0},{3,1},{4,6},{5,7},{6,4},{7,5},{8,10},{9,11},{10,... | collective-permute-start | bytes 1376264 | tf_op jit(solution)/shard_map/ppermute | solution.py:331
  12.5 21.7 %collective-permute-start.1 = (f32[14,64,128]{2,1,0:T(8,128)S(1)}, f32[14,64,128]{2,1,0:T(8,128)S(1)}, u32[]{:S(2)}, u32[]{:S(2)}) collective-permute-start(f32[14,64,128]{2,1,0:T(8,128)S(1)} %get-tuple-element.30.refs_0_), channel_id=1, source_target_pairs={{0,12},{1,13},{2,14},{3,15},{4,0},{5,1},{6,2},{7,3},{8,4},{9,5},{1... | collective-permute-start | bytes 1376264 | tf_op jit(solution)/shard_map/ppermute | solution.py:331
  16.1 27.1 %collective-permute-start = (f32[14,64,128]{2,1,0:T(8,128)S(1)}, f32[14,64,128]{2,1,0:T(8,128)S(1)}, u32[]{:S(2)}, u32[]{:S(2)}) collective-permute-start(f32[14,64,128]{2,1,0:T(8,128)S(1)} %get-tuple-element.30.refs_0_), channel_id=1, source_target_pairs={{0,4},{1,5},{2,6},{3,7},{4,8},{5,9},{6,10},{7,11},{8,12},{9,13},{1... | collective-permute-start | bytes 1376264 | tf_op jit(solution)/shard_map/ppermute | solution.py:331
  30.5 27.9 %copy-start.16 = (f32[14,64,128]{2,1,0:T(8,128)}, f32[14,64,128]{2,1,0:T(8,128)S(1)}, u32[]{:S(2)}) copy-start(f32[14,64,128]{2,1,0:T(8,128)S(1)} %collective-permute-done.2.refs_4_) | copy-start | bytes 1376260
  34.2 37.9 %copy-start.7 = (f32[14,64,128]{2,1,0:T(8,128)}, f32[14,64,128]{2,1,0:T(8,128)S(1)}, u32[]{:S(2)}) copy-start(f32[14,64,128]{2,1,0:T(8,128)S(1)} %collective-permute-done.1.refs_3_) | copy-start | bytes 1376260
  43.3 13.4 %collective-permute-start.3 = (f32[14,64,128]{2,1,0:T(8,128)S(1)}, f32[14,64,128]{2,1,0:T(8,128)S(1)}, u32[]{:S(2)}, u32[]{:S(2)}) collective-permute-start(f32[14,64,128]{2,1,0:T(8,128)S(1)} %collective-permute-done.refs_2_.refs_1_), channel_id=1, source_target_pairs={{0,4},{1,5},{2,6},{3,7},{4,8},{5,9},{6,10},{7,11},{8,12},{9,13},{1... | collective-permute-start | bytes 1376264 | tf_op jit(solution)/shard_map/ppermute | solution.py:331
  44.1 14.3 %collective-permute-start.8 = (f32[14,64,128]{2,1,0:T(8,128)S(1)}, f32[14,64,128]{2,1,0:T(8,128)S(1)}, u32[]{:S(2)}, u32[]{:S(2)}) collective-permute-start(f32[14,64,128]{2,1,0:T(8,128)S(1)} %collective-permute-done.1.refs_3_), channel_id=1, source_target_pairs={{0,2},{1,3},{2,0},{3,1},{4,6},{5,7},{6,4},{7,5},{8,10},{9,11},{10,... | collective-permute-start | bytes 1376264 | tf_op jit(solution)/shard_map/ppermute | solution.py:331
  46.0 28.3 %copy-start.23 = (s32[16,8]{0,1:T(8,128)S(1)}, s32[16,8]{0,1:T(8,128)}, u32[]{:S(2)}) copy-start(s32[16,8]{0,1:T(8,128)} %param.21) | copy-start | bytes 1540
  46.0 28.3 %copy-start.14 = (s32[8,8]{1,0:T(8,128)S(1)}, s32[8,8]{1,0:T(8,128)}, u32[]{:S(2)}) copy-start(s32[8,8]{1,0:T(8,128)} %far_one.1) | copy-start | bytes 772
  46.0 28.3 %copy-start.15 = (s32[4,8]{1,0:T(4,128)S(1)}, s32[4,8]{1,0:T(4,128)}, u32[]{:S(2)}) copy-start(s32[4,8]{1,0:T(4,128)} %far_two.1) | copy-start | bytes 388
  56.7 15.4 %copy-start.9 = (f32[14,64,128]{2,1,0:T(8,128)}, f32[14,64,128]{2,1,0:T(8,128)S(1)}, u32[]{:S(2)}) copy-start(f32[14,64,128]{2,1,0:T(8,128)S(1)} %collective-permute-done.3.refs_1_.refs_2_) | copy-start | bytes 1376260
  56.7 16.0 %collective-permute-start.9 = (f32[14,64,128]{2,1,0:T(8,128)S(1)}, f32[14,64,128]{2,1,0:T(8,128)S(1)}, u32[]{:S(2)}, u32[]{:S(2)}) collective-permute-start(f32[14,64,128]{2,1,0:T(8,128)S(1)} %get-tuple-element.30.refs_0_), channel_id=1, source_target_pairs={{0,1},{1,0},{2,3},{3,2},{4,5},{5,4},{6,7},{7,6},{8,9},{9,8},{10,11... | collective-permute-start | bytes 1376264 | tf_op jit(solution)/shard_map/ppermute | solution.py:331
  57.0 16.1 %collective-permute-start.10 = (f32[14,64,128]{2,1,0:T(8,128)S(1)}, f32[14,64,128]{2,1,0:T(8,128)S(1)}, u32[]{:S(2)}, u32[]{:S(2)}) collective-permute-start(f32[14,64,128]{2,1,0:T(8,128)S(1)} %collective-permute-done.refs_2_.refs_1_), channel_id=1, source_target_pairs={{0,1},{1,0},{2,3},{3,2},{4,5},{5,4},{6,7},{7,6},{8,9},{9,8},{10,11... | collective-permute-start | bytes 1376264 | tf_op jit(solution)/shard_map/ppermute | solution.py:331
  57.2 14.9 %collective-permute-start.7 = (f32[14,64,128]{2,1,0:T(8,128)S(1)}, f32[14,64,128]{2,1,0:T(8,128)}, u32[]{:S(2)}, u32[]{:S(2)}) collective-permute-start(f32[14,64,128]{2,1,0:T(8,128)S(1)} %collective-permute-done.3.refs_1_.refs_2_), channel_id=1, source_target_pairs={{0,2},{1,3},{2,0},{3,1},{4,6},{5,7},{6,4},{7,5},{8,10},{9,11},{10,... | collective-permute-start | bytes 1376264 | tf_op jit(solution)/shard_map/ppermute | solution.py:331
  58.0 14.1 %collective-permute-start.6 = (f32[14,64,128]{2,1,0:T(8,128)S(1)}, f32[14,64,128]{2,1,0:T(8,128)}, u32[]{:S(2)}, u32[]{:S(2)}) collective-permute-start(f32[14,64,128]{2,1,0:T(8,128)S(1)} %collective-permute-done.2.refs_4_), channel_id=1, source_target_pairs={{0,4},{1,5},{2,6},{3,7},{4,8},{5,9},{6,10},{7,11},{8,12},{9,13},{1... | collective-permute-start | bytes 1376264 | tf_op jit(solution)/shard_map/ppermute | solution.py:331
  58.4 14.2 %collective-permute-start.13 = (f32[14,64,128]{2,1,0:T(8,128)S(1)}, f32[14,64,128]{2,1,0:T(8,128)S(1)}, u32[]{:S(2)}, u32[]{:S(2)}) collective-permute-start(f32[14,64,128]{2,1,0:T(8,128)S(1)} %collective-permute-done.2.refs_4_), channel_id=1, source_target_pairs={{0,1},{1,0},{2,3},{3,2},{4,5},{5,4},{6,7},{7,6},{8,9},{9,8},{10,11... | collective-permute-start | bytes 1376264 | tf_op jit(solution)/shard_map/ppermute | solution.py:331
  72.1 2.9 %collective-permute-start.12 = (f32[14,64,128]{2,1,0:T(8,128)S(1)}, f32[14,64,128]{2,1,0:T(8,128)}, u32[]{:S(2)}, u32[]{:S(2)}) collective-permute-start(f32[14,64,128]{2,1,0:T(8,128)S(1)} %collective-permute-done.1.refs_3_), channel_id=1, source_target_pairs={{0,1},{1,0},{2,3},{3,2},{4,5},{5,4},{6,7},{7,6},{8,9},{9,8},{10,11... | collective-permute-start | bytes 1376264 | tf_op jit(solution)/shard_map/ppermute | solution.py:331
  72.1 3.2 %collective-permute-start.11 = (f32[14,64,128]{2,1,0:T(8,128)S(1)}, f32[14,64,128]{2,1,0:T(8,128)}, u32[]{:S(2)}, u32[]{:S(2)}) collective-permute-start(f32[14,64,128]{2,1,0:T(8,128)S(1)} %collective-permute-done.3.refs_1_.refs_2_), channel_id=1, source_target_pairs={{0,1},{1,0},{2,3},{3,2},{4,5},{5,4},{6,7},{7,6},{8,9},{9,8},{10,11... | collective-permute-start | bytes 1376264 | tf_op jit(solution)/shard_map/ppermute | solution.py:331
  72.6 2.8 %collective-permute-start.14 = (f32[14,64,128]{2,1,0:T(8,128)}, f32[14,64,128]{2,1,0:T(8,128)S(1)}, u32[]{:S(2)}, u32[]{:S(2)}) collective-permute-start(f32[14,64,128]{2,1,0:T(8,128)} %collective-permute-done.6.refs_5_), channel_id=1, source_target_pairs={{0,1},{1,0},{2,3},{3,2},{4,5},{5,4},{6,7},{7,6},{8,9},{9,8},{10,11... | collective-permute-start | bytes 1376264 | tf_op jit(solution)/shard_map/ppermute | solution.py:331
  72.7 3.4 %collective-permute-start.15 = (f32[14,64,128]{2,1,0:T(8,128)}, f32[14,64,128]{2,1,0:T(8,128)S(1)}, u32[]{:S(2)}, u32[]{:S(2)}) collective-permute-start(f32[14,64,128]{2,1,0:T(8,128)} %collective-permute-done.7.refs_6_), channel_id=1, source_target_pairs={{0,1},{1,0},{2,3},{3,2},{4,5},{5,4},{6,7},{7,6},{8,9},{9,8},{10,11... | collective-permute-start | bytes 1376264 | tf_op jit(solution)/shard_map/ppermute | solution.py:331
  74.2 2.5 %collective-permute-start.16 = (f32[14,64,128]{2,1,0:T(8,128)S(1)}, f32[14,64,128]{2,1,0:T(8,128)}, u32[]{:S(2)}, u32[]{:S(2)}) collective-permute-start(f32[14,64,128]{2,1,0:T(8,128)S(1)} %collective-permute-done.8.refs_7_), channel_id=1, source_target_pairs={{0,1},{1,0},{2,3},{3,2},{4,5},{5,4},{6,7},{7,6},{8,9},{9,8},{10,11... | collective-permute-start | bytes 1376264 | tf_op jit(solution)/shard_map/ppermute | solution.py:331
  (17 other events, 63.1 us)

commit v4 on v3

--- a/solution.py
+++ b/solution.py
@@ -14,8 +14,8 @@
 TINY = 1e-10
 NN = (((1,), (0,)), ((), ()))
 NT = (((1,), (1,)), ((), ()))
-GROUP = 8
-NEAR_WORK = 10**10
+GROUP = 16
+NEAR_WORK = 10**6
 OWN_WORK = 10**6
 NEAR_MEBIBYTES = 16
 DOWN_MEBIBYTES = 56
@@ -238,13 +238,15 @@
         pieces = []
         for k in range(0, partner_count, 2):
             even, odd = codes[node, k], codes[node, k + 1]
-            left = pltpu.roll(table[even // 2], (even % 2) * rank, 1)
-            right = pltpu.roll(table[odd // 2], (1 - odd % 2) * rank, 1)
-            pieces.append(jnp.where(lane < rank, left, right))
+            left, right = table[even // 2], table[odd // 2]
+            straight = jnp.where(lane < rank, left, right)
+            turned = pltpu.roll(jnp.where(lane < rank, right, left), rank, 1)
+            other = jnp.where(lane < rank, even % 2, 1 - odd % 2)
+            pieces.append(jnp.where(other == 0, straight, turned))
         return product(jnp.concatenate(pieces, axis=1), coupling, NT)
 
     def level(base, coupling):
-        width = min(4, coupling.shape[0] // 2)
+        width = min(8, coupling.shape[0] // 2)
 
         def step(i, carry):
             for j in range(width):

time: 88.2 us -> 85.9 us (0.974)
  waiting for transfers between devices: 28.5 us -> 25.4 us
    ppermute x15, waiting for transfers between devices: 28.5 us -> 25.4 us  [swap(): return lax.ppermute(value, 'leaf', pairs)]
    pallas_call x3, Pallas kernels: 25.5 us -> 26.6 us  [near_field(): pl.pallas_call(functools.partial(near_kernel, which, part, leaves), out_s...]
    pallas_call x1, Pallas kernels: 10.8 us -> 9.91 us  [on_device(): pl.pallas_call(down_kernel, out_shape=jax.ShapeDtypeStruct(input_vectors....]
    unnamed x49 -> x51, local copies, waits for them, and re-layouts: 6.67 us -> 7.14 us
  transfers between devices with their start and end apart: 17 -> 17, of which waited for: 9 -> 7; matrix products, arithmetic and copies ran while one was open for 0% -> 0% of each run, Pallas kernels for 30% -> 33%
where the time goes in v4:
time: 85.9 us; the launch traced here: 85.2 us
  Pallas kernels  37.8 us (44%)
  waiting for transfers between devices  25.4 us (30%)
  starting transfers between devices  14.5 us (17%)
  local copies, waits for them, and re-layouts  7.14 us (8%)
    pallas_call x3, Pallas kernels, near_field(): pl.pallas_call(functools.partial(near_kernel, which, part, leaves), out_s...  26.6 us
    ppermute x15, waiting for transfers between devices, swap(): return lax.ppermute(value, 'leaf', pairs)  25.4 us
    ppermute x15, starting transfers between devices, swap(): return lax.ppermute(value, 'leaf', pairs)  9.99 us
    pallas_call x1, Pallas kernels, on_device(): pl.pallas_call(down_kernel, out_shape=jax.ShapeDtypeStruct(input_vectors....  9.91 us
    unnamed x51, local copies, waits for them, and re-layouts  7.14 us
    ppermute x1, starting transfers between devices, on_device(): from_before = lax.ppermute(stacked, 'leaf', before)  3.1 us
  transfers between devices with their start and end apart: 17, of which 7 were waited for; matrix products, arithmetic and copies ran while one was open for 0% of the time, Pallas kernels for 33%

profile of v4, /device:TPU:0, one launch (start us, length us, event | category | flops | bytes accessed | tf_op | source)
XLA Modules:
  0.0 85.2 jit_solution(8777480414280628909)
XLA Ops:
  0.0 1.2 %copy-done = f32[64,4096]{1,0:T(8,128)S(1)} copy-done((f32[64,4096]{1,0:T(8,128)S(1)}, f32[64,4096]{1,0:T(8,128)}, u32[]{:S(2)}) %copy-start) | copy-done | bytes 1048600
  1.2 0.8 copy-done.8
  2.2 1.4 %collective-permute-start.5 = (f32[64,4352]{1,0:T(8,128)S(1)}, f32[64,4352]{1,0:T(8,128)S(1)}, u32[]{:S(2)}, u32[]{:S(2)}) collective-permute-start(f32[64,4352]{1,0:T(8,128)S(1)} %pack.1._.block), channel_id=1, source_target_pairs={{1,0},{2,1},{3,2},{4,3},{5,4},{6,5},{7,6},{8,7},{9,8},{10,9},{11,1... | collective-permute-start | bytes 3342344 | tf_op jit(solution)/shard_map/ppermute | solution.py:323
  3.6 3.1 %collective-permute-start.4 = (f32[64,4352]{1,0:T(8,128)S(1)}, f32[64,4352]{1,0:T(8,128)S(1)}, u32[]{:S(2)}, u32[]{:S(2)}) collective-permute-start(f32[64,4352]{1,0:T(8,128)S(1)} %pack.1._.block), channel_id=1, source_target_pairs={{0,1},{1,2},{2,3},{3,4},{4,5},{5,6},{6,7},{7,8},{8,9},{9,10},{10,1... | collective-permute-start | bytes 3342344 | tf_op jit(solution)/shard_map/ppermute | solution.py:322
  6.8 0.9 %copy-done.7 = f32[8,64,128]{2,1,0:T(8,128)S(1)} copy-done((f32[8,64,128]{2,1,0:T(8,128)S(1)}, f32[8,64,128]{2,1,0:T(8,128)}, u32[]{:S(2)}) %copy-start.7) | copy-done | bytes 262168
  7.7 0.9 %copy-done.10 = f32[4,64,128]{2,1,0:T(8,128)S(1)} copy-done((f32[4,64,128]{2,1,0:T(8,128)S(1)}, f32[4,64,128]{2,1,0:T(8,128)}, u32[]{:S(2)}) %copy-start.10) | copy-done | bytes 131096
  8.6 1.1 %up.1 = (f32[14,64,128]{2,1,0:T(8,128)S(1)}, s32[6,256]{1,0:T(8,128)S(1)}) custom-call(s32[16,16]{1,0:T(8,128)S(1)} %copy-done.13, f32[64,4096]{1,0:T(8,128)S(1)} %copy-done.1, f32[16,64,256]{2,1,0:T(8,128)S(1)} %copy-done.2, f32[8,64,128]{2,1,0:T(8,128)S(1)} %copy-done.7, f32[4,64,128]{2,1,0:T(8,128)S(1)} %copy-done.10, f32[64,4352]{1,0:T(8,128)S(1)} %pack.1._.block), custom_call_target="tpu_custom_call" | custom-call | tf_op jit(solution)/shard_map/up/pallas_call | solution.py:338
  9.7 3.0 %collective-permute-start.2 = (f32[14,64,128]{2,1,0:T(8,128)S(1)}, f32[14,64,128]{2,1,0:T(8,128)S(1)}, u32[]{:S(2)}, u32[]{:S(2)}) collective-permute-start(f32[14,64,128]{2,1,0:T(8,128)S(1)} %get-tuple-element.30.refs_0_), channel_id=1, source_target_pairs={{0,2},{1,3},{2,0},{3,1},{4,6},{5,7},{6,4},{7,5},{8,10},{9,11},{10,... | collective-permute-start | bytes 1376264 | tf_op jit(solution)/shard_map/ppermute | solution.py:333
  12.7 3.7 %collective-permute-start.1 = (f32[14,64,128]{2,1,0:T(8,128)S(1)}, f32[14,64,128]{2,1,0:T(8,128)S(1)}, u32[]{:S(2)}, u32[]{:S(2)}) collective-permute-start(f32[14,64,128]{2,1,0:T(8,128)S(1)} %get-tuple-element.30.refs_0_), channel_id=1, source_target_pairs={{0,12},{1,13},{2,14},{3,15},{4,0},{5,1},{6,2},{7,3},{8,4},{9,5},{1... | collective-permute-start | bytes 1376264 | tf_op jit(solution)/shard_map/ppermute | solution.py:333
  16.4 14.3 %near_own.1.refs_0_ = f32[64,4096]{1,0:T(8,128)S(1)} custom-call(s32[6,256]{1,0:T(8,128)S(1)} %get-tuple-element.25.lists, f32[3,4096]{1,0:T(4,128)S(1)} %copy-done.9, f32[64,4352]{1,0:T(8,128)S(1)} %pack.1._.block), custom_call_target="tpu_custom_call" | custom-call | flops 1000000 | bytes 3145728 | tf_op jit(solution)/shard_map/near_own/pallas_call | solution.py:360
  30.7 3.2 %collective-permute-done.1.refs_3_ = f32[14,64,128]{2,1,0:T(8,128)S(1)} collective-permute-done((f32[14,64,128]{2,1,0:T(8,128)S(1)}, f32[14,64,128]{2,1,0:T(8,128)S(1)}, u32[]{:S(2)}, u32[]{:S(2)}) %collective-permute-start.1) | collective-permute-done | bytes 458784 | tf_op jit(solution)/shard_map/ppermute | solution.py:333
  33.9 9.3 %collective-permute-done.refs_2_.refs_1_ = f32[14,64,128]{2,1,0:T(8,128)S(1)} collective-permute-done((f32[14,64,128]{2,1,0:T(8,128)S(1)}, f32[14,64,128]{2,1,0:T(8,128)S(1)}, u32[]{:S(2)}, u32[]{:S(2)}) %collective-permute-start) | collective-permute-done | bytes 458784 | tf_op jit(solution)/shard_map/ppermute | solution.py:333
  43.3 0.8 collective-permute-start.3
  44.1 1.9 %near_before.1.refs_0_ = f32[64,4096]{1,0:T(8,128)S(1)} custom-call(s32[6,256]{1,0:T(8,128)S(1)} %get-tuple-element.25.lists, f32[3,4096]{1,0:T(4,128)S(1)} %copy-done.9, f32[64,4352]{1,0:T(8,128)S(1)} %collective-permute-done.4.block, f32[64,4096]{1,0:T(8,128)S(1)} %near_own.1.refs_0_, f32[64,4352]{1,0:T(8,128)S(1)} %collective-permute-done.5.refs_1_.block, ...), custom_call_target="tpu_custom_call" | custom-call | flops 1000000 | bytes 3145728 | tf_op jit(solution)/shard_map/near_before/pallas_call | solution.py:360
  46.0 10.7 %collective-permute-done.3.refs_1_.refs_2_ = f32[14,64,128]{2,1,0:T(8,128)S(1)} collective-permute-done((f32[14,64,128]{2,1,0:T(8,128)S(1)}, f32[14,64,128]{2,1,0:T(8,128)S(1)}, u32[]{:S(2)}, u32[]{:S(2)}) %collective-permute-start.3) | collective-permute-done | bytes 458784 | tf_op jit(solution)/shard_map/ppermute | solution.py:333
  56.7 0.6 collective-permute-start.13
  57.9 10.4 %near_after.1.refs_22_ = f32[64,4096]{1,0:T(8,128)S(1)} custom-call(s32[6,256]{1,0:T(8,128)S(1)} %get-tuple-element.25.lists, f32[3,4096]{1,0:T(4,128)S(1)} %copy-done.9, f32[64,4352]{1,0:T(8,128)S(1)} %collective-permute-done.5.refs_1_.block, f32[64,4096]{1,0:T(8,128)S(1)} %near_before.1.refs_0_, f32[14,64,128]{2,1,0:T(8,128)S(1)} %collective-permute-done.3.refs_1_.refs_2_), custom_call_target="tpu_custom_call" | custom-call | flops 1000000 | bytes 3145728 | tf_op jit(solution)/shard_map/near_after/pallas_call | solution.py:360
  68.4 1.0 %copy-done.3 = f32[64,4096]{1,0:T(8,128)} copy-done((f32[64,4096]{1,0:T(8,128)}, f32[64,4096]{1,0:T(8,128)S(1)}, u32[]{:S(2)}) %copy-start.3) | copy-done | bytes 1048600
  69.4 0.9 %collective-permute-done.6.refs_5_ = f32[14,64,128]{2,1,0:T(8,128)S(1)} collective-permute-done((f32[14,64,128]{2,1,0:T(8,128)S(1)}, f32[14,64,128]{2,1,0:T(8,128)S(1)}, u32[]{:S(2)}, u32[]{:S(2)}) %collective-permute-start.6) | collective-permute-done | bytes 458784 | tf_op jit(solution)/shard_map/ppermute | solution.py:333
  71.8 0.8 copy-done.21
  73.0 0.6 copy-done.12
  73.6 0.6 collective-permute-done.11.refs_10_
  74.3 0.6 collective-permute-done.16.refs_15_
  75.2 9.9 %down.1 = f32[64,4096]{1,0:T(8,128)} custom-call(s32[28,8]{1,0:T(8,128)} %copy-done.12, f32[14,64,128]{2,1,0:T(8,128)} %copy-done.11, f32[14,64,128]{2,1,0:T(8,128)} %copy-done.6, f32[14,64,128]{2,1,0:T(8,128)} %copy-done.4, f32[14,64,128]{2,1,0:T(8,128)} %copy-done.5, f32[14,64,128]{2,1,0:T(8,128)} %copy-done.16, f32[14,64,128]{2,1,0:T(8,128)} %copy-done.18, ...), custom_call_target="tpu_custom_call" | custom-call | tf_op jit(solution)/shard_map/down/pallas_call | solution.py:422
  (68 shorter events, 3.1 us)
Async XLA Ops:
  2.1 14.3 %copy-start.9 = (f32[3,4096]{1,0:T(4,128)S(1)}, f32[3,4096]{1,0:T(4,128)}, u32[]{:S(2)}) copy-start(f32[3,4096]{1,0:T(4,128)} %p_own.5) | copy-start | bytes 147460
  2.2 41.9 %collective-permute-start.5 = (f32[64,4352]{1,0:T(8,128)S(1)}, f32[64,4352]{1,0:T(8,128)S(1)}, u32[]{:S(2)}, u32[]{:S(2)}) collective-permute-start(f32[64,4352]{1,0:T(8,128)S(1)} %pack.1._.block), channel_id=1, source_target_pairs={{1,0},{2,1},{3,2},{4,3},{5,4},{6,5},{7,6},{8,7},{9,8},{10,9},{11,1... | collective-permute-start | bytes 3342344 | tf_op jit(solution)/shard_map/ppermute | solution.py:323
  3.6 40.5 %collective-permute-start.4 = (f32[64,4352]{1,0:T(8,128)S(1)}, f32[64,4352]{1,0:T(8,128)S(1)}, u32[]{:S(2)}, u32[]{:S(2)}) collective-permute-start(f32[64,4352]{1,0:T(8,128)S(1)} %pack.1._.block), channel_id=1, source_target_pairs={{0,1},{1,2},{2,3},{3,4},{4,5},{5,6},{6,7},{7,8},{8,9},{9,10},{10,1... | collective-permute-start | bytes 3342344 | tf_op jit(solution)/shard_map/ppermute | solution.py:322
  9.7 47.6 %copy-start.11 = (f32[14,64,128]{2,1,0:T(8,128)}, f32[14,64,128]{2,1,0:T(8,128)S(1)}, u32[]{:S(2)}) copy-start(f32[14,64,128]{2,1,0:T(8,128)S(1)} %get-tuple-element.30.refs_0_) | copy-start | bytes 1376260
  9.7 20.9 %collective-permute-start.2 = (f32[14,64,128]{2,1,0:T(8,128)S(1)}, f32[14,64,128]{2,1,0:T(8,128)S(1)}, u32[]{:S(2)}, u32[]{:S(2)}) collective-permute-start(f32[14,64,128]{2,1,0:T(8,128)S(1)} %get-tuple-element.30.refs_0_), channel_id=1, source_target_pairs={{0,2},{1,3},{2,0},{3,1},{4,6},{5,7},{6,4},{7,5},{8,10},{9,11},{10,... | collective-permute-start | bytes 1376264 | tf_op jit(solution)/shard_map/ppermute | solution.py:333
  12.7 21.2 %collective-permute-start.1 = (f32[14,64,128]{2,1,0:T(8,128)S(1)}, f32[14,64,128]{2,1,0:T(8,128)S(1)}, u32[]{:S(2)}, u32[]{:S(2)}) collective-permute-start(f32[14,64,128]{2,1,0:T(8,128)S(1)} %get-tuple-element.30.refs_0_), channel_id=1, source_target_pairs={{0,12},{1,13},{2,14},{3,15},{4,0},{5,1},{6,2},{7,3},{8,4},{9,5},{1... | collective-permute-start | bytes 1376264 | tf_op jit(solution)/shard_map/ppermute | solution.py:333
  16.4 26.9 %collective-permute-start = (f32[14,64,128]{2,1,0:T(8,128)S(1)}, f32[14,64,128]{2,1,0:T(8,128)S(1)}, u32[]{:S(2)}, u32[]{:S(2)}) collective-permute-start(f32[14,64,128]{2,1,0:T(8,128)S(1)} %get-tuple-element.30.refs_0_), channel_id=1, source_target_pairs={{0,4},{1,5},{2,6},{3,7},{4,8},{5,9},{6,10},{7,11},{8,12},{9,13},{1... | collective-permute-start | bytes 1376264 | tf_op jit(solution)/shard_map/ppermute | solution.py:333
  30.7 26.0 %copy-start.16 = (f32[14,64,128]{2,1,0:T(8,128)}, f32[14,64,128]{2,1,0:T(8,128)S(1)}, u32[]{:S(2)}) copy-start(f32[14,64,128]{2,1,0:T(8,128)S(1)} %collective-permute-done.2.refs_4_) | copy-start | bytes 1376260
  33.9 36.3 %copy-start.5 = (f32[14,64,128]{2,1,0:T(8,128)}, f32[14,64,128]{2,1,0:T(8,128)S(1)}, u32[]{:S(2)}) copy-start(f32[14,64,128]{2,1,0:T(8,128)S(1)} %collective-permute-done.1.refs_3_) | copy-start | bytes 1376260
  43.3 13.4 %collective-permute-start.3 = (f32[14,64,128]{2,1,0:T(8,128)S(1)}, f32[14,64,128]{2,1,0:T(8,128)S(1)}, u32[]{:S(2)}, u32[]{:S(2)}) collective-permute-start(f32[14,64,128]{2,1,0:T(8,128)S(1)} %collective-permute-done.refs_2_.refs_1_), channel_id=1, source_target_pairs={{0,4},{1,5},{2,6},{3,7},{4,8},{5,9},{6,10},{7,11},{8,12},{9,13},{1... | collective-permute-start | bytes 1376264 | tf_op jit(solution)/shard_map/ppermute | solution.py:333
  44.1 13.4 %collective-permute-start.8 = (f32[14,64,128]{2,1,0:T(8,128)S(1)}, f32[14,64,128]{2,1,0:T(8,128)S(1)}, u32[]{:S(2)}, u32[]{:S(2)}) collective-permute-start(f32[14,64,128]{2,1,0:T(8,128)S(1)} %collective-permute-done.1.refs_3_), channel_id=1, source_target_pairs={{0,2},{1,3},{2,0},{3,1},{4,6},{5,7},{6,4},{7,5},{8,10},{9,11},{10,... | collective-permute-start | bytes 1376264 | tf_op jit(solution)/shard_map/ppermute | solution.py:333
  46.0 26.9 %copy-start.24 = (s32[16,8]{0,1:T(8,128)S(1)}, s32[16,8]{0,1:T(8,128)}, u32[]{:S(2)}) copy-start(s32[16,8]{0,1:T(8,128)} %param.21) | copy-start | bytes 1540
  46.0 26.9 %copy-start.14 = (s32[8,8]{1,0:T(8,128)S(1)}, s32[8,8]{1,0:T(8,128)}, u32[]{:S(2)}) copy-start(s32[8,8]{1,0:T(8,128)} %far_one.1) | copy-start | bytes 772
  46.0 26.9 %copy-start.15 = (s32[4,8]{1,0:T(4,128)S(1)}, s32[4,8]{1,0:T(4,128)}, u32[]{:S(2)}) copy-start(s32[4,8]{1,0:T(4,128)} %far_two.1) | copy-start | bytes 388
  56.7 13.6 %collective-permute-start.6 = (f32[14,64,128]{2,1,0:T(8,128)S(1)}, f32[14,64,128]{2,1,0:T(8,128)S(1)}, u32[]{:S(2)}, u32[]{:S(2)}) collective-permute-start(f32[14,64,128]{2,1,0:T(8,128)S(1)} %collective-permute-done.2.refs_4_), channel_id=1, source_target_pairs={{0,4},{1,5},{2,6},{3,7},{4,8},{5,9},{6,10},{7,11},{8,12},{9,13},{1... | collective-permute-start | bytes 1376264 | tf_op jit(solution)/shard_map/ppermute | solution.py:333
  56.7 13.6 %collective-permute-start.7 = (f32[14,64,128]{2,1,0:T(8,128)S(1)}, f32[14,64,128]{2,1,0:T(8,128)}, u32[]{:S(2)}, u32[]{:S(2)}) collective-permute-start(f32[14,64,128]{2,1,0:T(8,128)S(1)} %collective-permute-done.3.refs_1_.refs_2_), channel_id=1, source_target_pairs={{0,2},{1,3},{2,0},{3,1},{4,6},{5,7},{6,4},{7,5},{8,10},{9,11},{10,... | collective-permute-start | bytes 1376264 | tf_op jit(solution)/shard_map/ppermute | solution.py:333
  56.7 14.1 %collective-permute-start.13 = (f32[14,64,128]{2,1,0:T(8,128)S(1)}, f32[14,64,128]{2,1,0:T(8,128)S(1)}, u32[]{:S(2)}, u32[]{:S(2)}) collective-permute-start(f32[14,64,128]{2,1,0:T(8,128)S(1)} %collective-permute-done.2.refs_4_), channel_id=1, source_target_pairs={{0,1},{1,0},{2,3},{3,2},{4,5},{5,4},{6,7},{7,6},{8,9},{9,8},{10,11... | collective-permute-start | bytes 1376264 | tf_op jit(solution)/shard_map/ppermute | solution.py:333
  57.4 13.5 %collective-permute-start.9 = (f32[14,64,128]{2,1,0:T(8,128)S(1)}, f32[14,64,128]{2,1,0:T(8,128)S(1)}, u32[]{:S(2)}, u32[]{:S(2)}) collective-permute-start(f32[14,64,128]{2,1,0:T(8,128)S(1)} %get-tuple-element.30.refs_0_), channel_id=1, source_target_pairs={{0,1},{1,0},{2,3},{3,2},{4,5},{5,4},{6,7},{7,6},{8,9},{9,8},{10,11... | collective-permute-start | bytes 1376264 | tf_op jit(solution)/shard_map/ppermute | solution.py:333
  57.4 13.9 %collective-permute-start.10 = (f32[14,64,128]{2,1,0:T(8,128)S(1)}, f32[14,64,128]{2,1,0:T(8,128)S(1)}, u32[]{:S(2)}, u32[]{:S(2)}) collective-permute-start(f32[14,64,128]{2,1,0:T(8,128)S(1)} %collective-permute-done.refs_2_.refs_1_), channel_id=1, source_target_pairs={{0,1},{1,0},{2,3},{3,2},{4,5},{5,4},{6,7},{7,6},{8,9},{9,8},{10,11... | collective-permute-start | bytes 1376264 | tf_op jit(solution)/shard_map/ppermute | solution.py:333
  70.3 3.4 %collective-permute-start.12 = (f32[14,64,128]{2,1,0:T(8,128)S(1)}, f32[14,64,128]{2,1,0:T(8,128)}, u32[]{:S(2)}, u32[]{:S(2)}) collective-permute-start(f32[14,64,128]{2,1,0:T(8,128)S(1)} %collective-permute-done.1.refs_3_), channel_id=1, source_target_pairs={{0,1},{1,0},{2,3},{3,2},{4,5},{5,4},{6,7},{7,6},{8,9},{9,8},{10,11... | collective-permute-start | bytes 1376264 | tf_op jit(solution)/shard_map/ppermute | solution.py:333
  70.3 3.9 %collective-permute-start.11 = (f32[14,64,128]{2,1,0:T(8,128)S(1)}, f32[14,64,128]{2,1,0:T(8,128)}, u32[]{:S(2)}, u32[]{:S(2)}) collective-permute-start(f32[14,64,128]{2,1,0:T(8,128)S(1)} %collective-permute-done.3.refs_1_.refs_2_), channel_id=1, source_target_pairs={{0,1},{1,0},{2,3},{3,2},{4,5},{5,4},{6,7},{7,6},{8,9},{9,8},{10,11... | collective-permute-start | bytes 1376264 | tf_op jit(solution)/shard_map/ppermute | solution.py:333
  70.8 3.4 %collective-permute-start.14 = (f32[14,64,128]{2,1,0:T(8,128)S(1)}, f32[14,64,128]{2,1,0:T(8,128)S(1)}, u32[]{:S(2)}, u32[]{:S(2)}) collective-permute-start(f32[14,64,128]{2,1,0:T(8,128)S(1)} %collective-permute-done.6.refs_5_), channel_id=1, source_target_pairs={{0,1},{1,0},{2,3},{3,2},{4,5},{5,4},{6,7},{7,6},{8,9},{9,8},{10,11... | collective-permute-start | bytes 1376264 | tf_op jit(solution)/shard_map/ppermute | solution.py:333
  70.9 3.4 %collective-permute-start.15 = (f32[14,64,128]{2,1,0:T(8,128)}, f32[14,64,128]{2,1,0:T(8,128)S(1)}, u32[]{:S(2)}, u32[]{:S(2)}) collective-permute-start(f32[14,64,128]{2,1,0:T(8,128)} %collective-permute-done.7.refs_6_), channel_id=1, source_target_pairs={{0,1},{1,0},{2,3},{3,2},{4,5},{5,4},{6,7},{7,6},{8,9},{9,8},{10,11... | collective-permute-start | bytes 1376264 | tf_op jit(solution)/shard_map/ppermute | solution.py:333
  72.5 2.3 %collective-permute-start.16 = (f32[14,64,128]{2,1,0:T(8,128)S(1)}, f32[14,64,128]{2,1,0:T(8,128)}, u32[]{:S(2)}, u32[]{:S(2)}) collective-permute-start(f32[14,64,128]{2,1,0:T(8,128)S(1)} %collective-permute-done.8.refs_7_), channel_id=1, source_target_pairs={{0,1},{1,0},{2,3},{3,2},{4,5},{5,4},{6,7},{7,6},{8,9},{9,8},{10,11... | collective-permute-start | bytes 1376264 | tf_op jit(solution)/shard_map/ppermute | solution.py:333
  (18 other events, 69.8 us)

commit v5 on v4

--- a/solution.py
+++ b/solution.py
@@ -214,13 +214,13 @@
 
 
 def down_kernel(codes, *refs):
-    slots = refs[:-17]
-    sources, out = refs[-17:-10], refs[-10]
-    table, fields, *held, sems = refs[-9:]
+    slots = refs[:-18]
+    sources, out = refs[-18:-11], refs[-11]
+    table, fields, *held, total, sems = refs[-10:]
     second, c_two, c_one, c_zero, first, basis = held
     units = slots[0].shape[0]
     targets = [table.at[pl.ds(i * units, units)] for i in range(len(slots))]
-    targets += held + [out]
+    targets += held + [total]
     copies = [
         pltpu.make_async_copy(source, target, sems.at[i])
         for i, (source, target) in enumerate(zip(slots + sources, targets))
@@ -266,7 +266,7 @@
     for copy in copies[len(slots) + 4 :]:
         copy.wait()
 
-    ones = []
+    ones, results = [], []
     for p in range(leaves // 4):
         pair = fields[leaves // 2 + leaves // 4 + p // 2]
         top = pair[:, :rank] if p % 2 == 0 else pair[:, rank:]
@@ -279,7 +279,13 @@
             leaf = 2 * p + half
             low = zeros[:, :rank] if half == 0 else zeros[:, rank:]
             cut = slice(leaf * size, (leaf + 1) * size)
-            out[:, cut] += narrow(product(low, basis[leaf], NN))
+            total[:, cut] += narrow(product(low, basis[leaf], NN))
+        done = pl.ds(2 * p * size, 2 * size)
+        there = pltpu.make_async_copy(total.at[:, done], out.at[:, done], sems.at[p])
+        there.start()
+        results.append(there)
+    for there in results:
+        there.wait()
 
 
 def whole_vmem(n):
@@ -424,13 +430,13 @@
         out_shape=jax.ShapeDtypeStruct(input_vectors.shape, jnp.float32),
         in_specs=[pl.BlockSpec(memory_space=pltpu.SMEM)]
         + [pl.BlockSpec(memory_space=pl.ANY)] * copied,
-        out_specs=pl.BlockSpec(memory_space=pltpu.VMEM),
+        out_specs=pl.BlockSpec(memory_space=pl.ANY),
         scratch_shapes=[
             pltpu.VMEM((devices * units, rhs, 2 * rank), jnp.float32),
             pltpu.VMEM((units, rhs, 2 * rank), jnp.float32),
         ]
         + [pltpu.VMEM(operand.shape, jnp.float32) for operand in operands]
-        + [pltpu.SemaphoreType.DMA((copied,))],
+        + [pltpu.VMEM(near.shape, jnp.float32), pltpu.SemaphoreType.DMA((copied,))],
         compiler_params=params(DOWN_MEBIBYTES),
         name="down",
     )(codes, *slots, *operands, near)

time: 85.9 us -> 85.2 us (level)
  Pallas kernels: 37.8 us -> 35.4 us
  waiting for transfers between devices: 25.4 us -> 26.7 us
    pallas_call x3, Pallas kernels: 26.6 us -> 24.5 us  [near_field(): pl.pallas_call(functools.partial(near_kernel, which, part, leaves), out_s...]
    ppermute x15, waiting for transfers between devices: 25.4 us -> 26.7 us  [swap(): return lax.ppermute(value, 'leaf', pairs)]
  transfers between devices with their start and end apart: 17 -> 17, of which waited for: 7 -> 7; matrix products, arithmetic and copies ran while one was open for 0% -> 0% of each run, Pallas kernels for 33% -> 30%
where the time goes in v5:
time: 85.2 us; the launch traced here: 84.8 us
  Pallas kernels  35.4 us (42%)
  waiting for transfers between devices  26.7 us (31%)
  starting transfers between devices  15.1 us (18%)
  local copies, waits for them, and re-layouts  7.25 us (9%)
    ppermute x15, waiting for transfers between devices, swap(): return lax.ppermute(value, 'leaf', pairs)  26.7 us
    pallas_call x3, Pallas kernels, near_field(): pl.pallas_call(functools.partial(near_kernel, which, part, leaves), out_s...  24.5 us
    ppermute x15, starting transfers between devices, swap(): return lax.ppermute(value, 'leaf', pairs)  10.6 us
    pallas_call x1, Pallas kernels, on_device(): pl.pallas_call(down_kernel, out_shape=jax.ShapeDtypeStruct(input_vectors....  9.6 us
    unnamed x51, local copies, waits for them, and re-layouts  7.25 us
    ppermute x1, starting transfers between devices, on_device(): from_before = lax.ppermute(stacked, 'leaf', before)  3.1 us
  transfers between devices with their start and end apart: 17, of which 7 were waited for; matrix products, arithmetic and copies ran while one was open for 0% of the time, Pallas kernels for 30%

profile of v5, /device:TPU:0, one launch (start us, length us, event | category | flops | bytes accessed | tf_op | source)
XLA Modules:
  0.0 84.8 jit_solution(6720883862368758063)
XLA Ops:
  0.0 1.2 %copy-done = f32[64,4096]{1,0:T(8,128)S(1)} copy-done((f32[64,4096]{1,0:T(8,128)S(1)}, f32[64,4096]{1,0:T(8,128)}, u32[]{:S(2)}) %copy-start) | copy-done | bytes 1048600
  1.2 0.8 copy-done.8
  2.2 1.4 %collective-permute-start.5 = (f32[64,4352]{1,0:T(8,128)S(1)}, f32[64,4352]{1,0:T(8,128)S(1)}, u32[]{:S(2)}, u32[]{:S(2)}) collective-permute-start(f32[64,4352]{1,0:T(8,128)S(1)} %pack.1._.block), channel_id=1, source_target_pairs={{1,0},{2,1},{3,2},{4,3},{5,4},{6,5},{7,6},{8,7},{9,8},{10,9},{11,1... | collective-permute-start | bytes 3342344 | tf_op jit(solution)/shard_map/ppermute | solution.py:329
  3.6 3.1 %collective-permute-start.4 = (f32[64,4352]{1,0:T(8,128)S(1)}, f32[64,4352]{1,0:T(8,128)S(1)}, u32[]{:S(2)}, u32[]{:S(2)}) collective-permute-start(f32[64,4352]{1,0:T(8,128)S(1)} %pack.1._.block), channel_id=1, source_target_pairs={{0,1},{1,2},{2,3},{3,4},{4,5},{5,6},{6,7},{7,8},{8,9},{9,10},{10,1... | collective-permute-start | bytes 3342344 | tf_op jit(solution)/shard_map/ppermute | solution.py:328
  6.8 0.9 %copy-done.7 = f32[8,64,128]{2,1,0:T(8,128)S(1)} copy-done((f32[8,64,128]{2,1,0:T(8,128)S(1)}, f32[8,64,128]{2,1,0:T(8,128)}, u32[]{:S(2)}) %copy-start.7) | copy-done | bytes 262168
  7.7 0.9 %copy-done.10 = f32[4,64,128]{2,1,0:T(8,128)S(1)} copy-done((f32[4,64,128]{2,1,0:T(8,128)S(1)}, f32[4,64,128]{2,1,0:T(8,128)}, u32[]{:S(2)}) %copy-start.10) | copy-done | bytes 131096
  8.6 1.1 %up.1 = (f32[14,64,128]{2,1,0:T(8,128)S(1)}, s32[6,256]{1,0:T(8,128)S(1)}) custom-call(s32[16,16]{1,0:T(8,128)S(1)} %copy-done.13, f32[64,4096]{1,0:T(8,128)S(1)} %copy-done.1, f32[16,64,256]{2,1,0:T(8,128)S(1)} %copy-done.2, f32[8,64,128]{2,1,0:T(8,128)S(1)} %copy-done.7, f32[4,64,128]{2,1,0:T(8,128)S(1)} %copy-done.10, f32[64,4352]{1,0:T(8,128)S(1)} %pack.1._.block), custom_call_target="tpu_custom_call" | custom-call | tf_op jit(solution)/shard_map/up/pallas_call | solution.py:344
  9.7 3.0 %collective-permute-start.2 = (f32[14,64,128]{2,1,0:T(8,128)S(1)}, f32[14,64,128]{2,1,0:T(8,128)S(1)}, u32[]{:S(2)}, u32[]{:S(2)}) collective-permute-start(f32[14,64,128]{2,1,0:T(8,128)S(1)} %get-tuple-element.30.refs_0_), channel_id=1, source_target_pairs={{0,2},{1,3},{2,0},{3,1},{4,6},{5,7},{6,4},{7,5},{8,10},{9,11},{10,... | collective-permute-start | bytes 1376264 | tf_op jit(solution)/shard_map/ppermute | solution.py:339
  12.7 3.7 %collective-permute-start.1 = (f32[14,64,128]{2,1,0:T(8,128)S(1)}, f32[14,64,128]{2,1,0:T(8,128)S(1)}, u32[]{:S(2)}, u32[]{:S(2)}) collective-permute-start(f32[14,64,128]{2,1,0:T(8,128)S(1)} %get-tuple-element.30.refs_0_), channel_id=1, source_target_pairs={{0,12},{1,13},{2,14},{3,15},{4,0},{5,1},{6,2},{7,3},{8,4},{9,5},{1... | collective-permute-start | bytes 1376264 | tf_op jit(solution)/shard_map/ppermute | solution.py:339
  16.4 12.2 %near_own.1.refs_0_ = f32[64,4096]{1,0:T(8,128)S(1)} custom-call(s32[6,256]{1,0:T(8,128)S(1)} %get-tuple-element.25.lists, f32[3,4096]{1,0:T(4,128)S(1)} %copy-done.9, f32[64,4352]{1,0:T(8,128)S(1)} %pack.1._.block), custom_call_target="tpu_custom_call" | custom-call | flops 1000000 | bytes 3145728 | tf_op jit(solution)/shard_map/near_own/pallas_call | solution.py:366
  28.6 1.9 %collective-permute-done.2.refs_4_ = f32[14,64,128]{2,1,0:T(8,128)S(1)} collective-permute-done((f32[14,64,128]{2,1,0:T(8,128)S(1)}, f32[14,64,128]{2,1,0:T(8,128)S(1)}, u32[]{:S(2)}, u32[]{:S(2)}) %collective-permute-start.2) | collective-permute-done | bytes 458784 | tf_op jit(solution)/shard_map/ppermute | solution.py:339
  30.5 3.4 %collective-permute-done.1.refs_3_ = f32[14,64,128]{2,1,0:T(8,128)S(1)} collective-permute-done((f32[14,64,128]{2,1,0:T(8,128)S(1)}, f32[14,64,128]{2,1,0:T(8,128)S(1)}, u32[]{:S(2)}, u32[]{:S(2)}) %collective-permute-start.1) | collective-permute-done | bytes 458784 | tf_op jit(solution)/shard_map/ppermute | solution.py:339
  33.9 9.3 %collective-permute-done.refs_2_.refs_1_ = f32[14,64,128]{2,1,0:T(8,128)S(1)} collective-permute-done((f32[14,64,128]{2,1,0:T(8,128)S(1)}, f32[14,64,128]{2,1,0:T(8,128)S(1)}, u32[]{:S(2)}, u32[]{:S(2)}) %collective-permute-start) | collective-permute-done | bytes 458784 | tf_op jit(solution)/shard_map/ppermute | solution.py:339
  43.3 0.8 collective-permute-start.3
  44.1 1.9 %near_before.1.refs_0_ = f32[64,4096]{1,0:T(8,128)S(1)} custom-call(s32[6,256]{1,0:T(8,128)S(1)} %get-tuple-element.25.lists, f32[3,4096]{1,0:T(4,128)S(1)} %copy-done.9, f32[64,4352]{1,0:T(8,128)S(1)} %collective-permute-done.4.block, f32[64,4096]{1,0:T(8,128)S(1)} %near_own.1.refs_0_, f32[64,4352]{1,0:T(8,128)S(1)} %collective-permute-done.5.refs_1_.block, ...), custom_call_target="tpu_custom_call" | custom-call | flops 1000000 | bytes 3145728 | tf_op jit(solution)/shard_map/near_before/pallas_call | solution.py:366
  46.0 10.7 %collective-permute-done.3.refs_1_.refs_2_ = f32[14,64,128]{2,1,0:T(8,128)S(1)} collective-permute-done((f32[14,64,128]{2,1,0:T(8,128)S(1)}, f32[14,64,128]{2,1,0:T(8,128)S(1)}, u32[]{:S(2)}, u32[]{:S(2)}) %collective-permute-start.3) | collective-permute-done | bytes 458784 | tf_op jit(solution)/shard_map/ppermute | solution.py:339
  56.7 1.3 %collective-permute-start.7 = (f32[14,64,128]{2,1,0:T(8,128)S(1)}, f32[14,64,128]{2,1,0:T(8,128)}, u32[]{:S(2)}, u32[]{:S(2)}) collective-permute-start(f32[14,64,128]{2,1,0:T(8,128)S(1)} %collective-permute-done.3.refs_1_.refs_2_), channel_id=1, source_target_pairs={{0,2},{1,3},{2,0},{3,1},{4,6},{5,7},{6,4},{7,5},{8,10},{9,11},{10,... | collective-permute-start | bytes 1376264 | tf_op jit(solution)/shard_map/ppermute | solution.py:339
  58.7 10.4 %near_after.1.refs_22_ = f32[64,4096]{1,0:T(8,128)S(1)} custom-call(s32[6,256]{1,0:T(8,128)S(1)} %get-tuple-element.25.lists, f32[3,4096]{1,0:T(4,128)S(1)} %copy-done.9, f32[64,4352]{1,0:T(8,128)S(1)} %collective-permute-done.5.refs_1_.block, f32[64,4096]{1,0:T(8,128)S(1)} %near_before.1.refs_0_, f32[14,64,128]{2,1,0:T(8,128)S(1)} %collective-permute-done.3.refs_1_.refs_2_), custom_call_target="tpu_custom_call" | custom-call | flops 1000000 | bytes 3145728 | tf_op jit(solution)/shard_map/near_after/pallas_call | solution.py:366
  69.1 1.0 %copy-done.3 = f32[64,4096]{1,0:T(8,128)} copy-done((f32[64,4096]{1,0:T(8,128)}, f32[64,4096]{1,0:T(8,128)S(1)}, u32[]{:S(2)}) %copy-start.3) | copy-done | bytes 1048600
  72.0 0.8 copy-done.21
  73.1 0.6 copy-done.12
  73.7 0.6 collective-permute-done.15.refs_14_
  74.3 0.6 collective-permute-done.16.refs_15_
  75.1 9.6 %down.1 = f32[64,4096]{1,0:T(8,128)} custom-call(s32[28,8]{1,0:T(8,128)} %copy-done.12, f32[14,64,128]{2,1,0:T(8,128)} %copy-done.11, f32[14,64,128]{2,1,0:T(8,128)} %copy-done.6, f32[14,64,128]{2,1,0:T(8,128)} %copy-done.4, f32[14,64,128]{2,1,0:T(8,128)} %copy-done.5, f32[14,64,128]{2,1,0:T(8,128)} %copy-done.16, f32[14,64,128]{2,1,0:T(8,128)} %copy-done.18, ...), custom_call_target="tpu_custom_call" | custom-call | tf_op jit(solution)/shard_map/down/pallas_call | solution.py:428
  (68 shorter events, 3.2 us)
Async XLA Ops:
  2.2 41.9 %collective-permute-start.5 = (f32[64,4352]{1,0:T(8,128)S(1)}, f32[64,4352]{1,0:T(8,128)S(1)}, u32[]{:S(2)}, u32[]{:S(2)}) collective-permute-start(f32[64,4352]{1,0:T(8,128)S(1)} %pack.1._.block), channel_id=1, source_target_pairs={{1,0},{2,1},{3,2},{4,3},{5,4},{6,5},{7,6},{8,7},{9,8},{10,9},{11,1... | collective-permute-start | bytes 3342344 | tf_op jit(solution)/shard_map/ppermute | solution.py:329
  3.6 40.5 %collective-permute-start.4 = (f32[64,4352]{1,0:T(8,128)S(1)}, f32[64,4352]{1,0:T(8,128)S(1)}, u32[]{:S(2)}, u32[]{:S(2)}) collective-permute-start(f32[64,4352]{1,0:T(8,128)S(1)} %pack.1._.block), channel_id=1, source_target_pairs={{0,1},{1,2},{2,3},{3,4},{4,5},{5,6},{6,7},{7,8},{8,9},{9,10},{10,1... | collective-permute-start | bytes 3342344 | tf_op jit(solution)/shard_map/ppermute | solution.py:328
  9.7 48.3 %copy-start.11 = (f32[14,64,128]{2,1,0:T(8,128)}, f32[14,64,128]{2,1,0:T(8,128)S(1)}, u32[]{:S(2)}) copy-start(f32[14,64,128]{2,1,0:T(8,128)S(1)} %get-tuple-element.30.refs_0_) | copy-start | bytes 1376260
  9.7 20.8 %collective-permute-start.2 = (f32[14,64,128]{2,1,0:T(8,128)S(1)}, f32[14,64,128]{2,1,0:T(8,128)S(1)}, u32[]{:S(2)}, u32[]{:S(2)}) collective-permute-start(f32[14,64,128]{2,1,0:T(8,128)S(1)} %get-tuple-element.30.refs_0_), channel_id=1, source_target_pairs={{0,2},{1,3},{2,0},{3,1},{4,6},{5,7},{6,4},{7,5},{8,10},{9,11},{10,... | collective-permute-start | bytes 1376264 | tf_op jit(solution)/shard_map/ppermute | solution.py:339
  12.7 21.2 %collective-permute-start.1 = (f32[14,64,128]{2,1,0:T(8,128)S(1)}, f32[14,64,128]{2,1,0:T(8,128)S(1)}, u32[]{:S(2)}, u32[]{:S(2)}) collective-permute-start(f32[14,64,128]{2,1,0:T(8,128)S(1)} %get-tuple-element.30.refs_0_), channel_id=1, source_target_pairs={{0,12},{1,13},{2,14},{3,15},{4,0},{5,1},{6,2},{7,3},{8,4},{9,5},{1... | collective-permute-start | bytes 1376264 | tf_op jit(solution)/shard_map/ppermute | solution.py:339
  16.4 26.9 %collective-permute-start = (f32[14,64,128]{2,1,0:T(8,128)S(1)}, f32[14,64,128]{2,1,0:T(8,128)S(1)}, u32[]{:S(2)}, u32[]{:S(2)}) collective-permute-start(f32[14,64,128]{2,1,0:T(8,128)S(1)} %get-tuple-element.30.refs_0_), channel_id=1, source_target_pairs={{0,4},{1,5},{2,6},{3,7},{4,8},{5,9},{6,10},{7,11},{8,12},{9,13},{1... | collective-permute-start | bytes 1376264 | tf_op jit(solution)/shard_map/ppermute | solution.py:339
  30.5 27.6 %copy-start.16 = (f32[14,64,128]{2,1,0:T(8,128)}, f32[14,64,128]{2,1,0:T(8,128)S(1)}, u32[]{:S(2)}) copy-start(f32[14,64,128]{2,1,0:T(8,128)S(1)} %collective-permute-done.2.refs_4_) | copy-start | bytes 1376260
  33.9 36.3 %copy-start.5 = (f32[14,64,128]{2,1,0:T(8,128)}, f32[14,64,128]{2,1,0:T(8,128)S(1)}, u32[]{:S(2)}) copy-start(f32[14,64,128]{2,1,0:T(8,128)S(1)} %collective-permute-done.1.refs_3_) | copy-start | bytes 1376260
  43.3 15.3 %copy-start.6 = (f32[14,64,128]{2,1,0:T(8,128)}, f32[14,64,128]{2,1,0:T(8,128)S(1)}, u32[]{:S(2)}) copy-start(f32[14,64,128]{2,1,0:T(8,128)S(1)} %collective-permute-done.refs_2_.refs_1_) | copy-start | bytes 1376260
  43.3 13.4 %collective-permute-start.3 = (f32[14,64,128]{2,1,0:T(8,128)S(1)}, f32[14,64,128]{2,1,0:T(8,128)S(1)}, u32[]{:S(2)}, u32[]{:S(2)}) collective-permute-start(f32[14,64,128]{2,1,0:T(8,128)S(1)} %collective-permute-done.refs_2_.refs_1_), channel_id=1, source_target_pairs={{0,4},{1,5},{2,6},{3,7},{4,8},{5,9},{6,10},{7,11},{8,12},{9,13},{1... | collective-permute-start | bytes 1376264 | tf_op jit(solution)/shard_map/ppermute | solution.py:339
  44.1 14.5 %collective-permute-start.8 = (f32[14,64,128]{2,1,0:T(8,128)S(1)}, f32[14,64,128]{2,1,0:T(8,128)S(1)}, u32[]{:S(2)}, u32[]{:S(2)}) collective-permute-start(f32[14,64,128]{2,1,0:T(8,128)S(1)} %collective-permute-done.1.refs_3_), channel_id=1, source_target_pairs={{0,2},{1,3},{2,0},{3,1},{4,6},{5,7},{6,4},{7,5},{8,10},{9,11},{10,... | collective-permute-start | bytes 1376264 | tf_op jit(solution)/shard_map/ppermute | solution.py:339
  46.0 26.9 %copy-start.24 = (s32[16,8]{0,1:T(8,128)S(1)}, s32[16,8]{0,1:T(8,128)}, u32[]{:S(2)}) copy-start(s32[16,8]{0,1:T(8,128)} %param.21) | copy-start | bytes 1540
  46.0 27.0 %copy-start.14 = (s32[8,8]{1,0:T(8,128)S(1)}, s32[8,8]{1,0:T(8,128)}, u32[]{:S(2)}) copy-start(s32[8,8]{1,0:T(8,128)} %far_one.1) | copy-start | bytes 772
  46.0 26.9 %copy-start.15 = (s32[4,8]{1,0:T(4,128)S(1)}, s32[4,8]{1,0:T(4,128)}, u32[]{:S(2)}) copy-start(s32[4,8]{1,0:T(4,128)} %far_two.1) | copy-start | bytes 388
  56.7 13.6 %collective-permute-start.6 = (f32[14,64,128]{2,1,0:T(8,128)S(1)}, f32[14,64,128]{2,1,0:T(8,128)S(1)}, u32[]{:S(2)}, u32[]{:S(2)}) collective-permute-start(f32[14,64,128]{2,1,0:T(8,128)S(1)} %collective-permute-done.2.refs_4_), channel_id=1, source_target_pairs={{0,4},{1,5},{2,6},{3,7},{4,8},{5,9},{6,10},{7,11},{8,12},{9,13},{1... | collective-permute-start | bytes 1376264 | tf_op jit(solution)/shard_map/ppermute | solution.py:339
  56.7 13.9 %collective-permute-start.7 = (f32[14,64,128]{2,1,0:T(8,128)S(1)}, f32[14,64,128]{2,1,0:T(8,128)}, u32[]{:S(2)}, u32[]{:S(2)}) collective-permute-start(f32[14,64,128]{2,1,0:T(8,128)S(1)} %collective-permute-done.3.refs_1_.refs_2_), channel_id=1, source_target_pairs={{0,2},{1,3},{2,0},{3,1},{4,6},{5,7},{6,4},{7,5},{8,10},{9,11},{10,... | collective-permute-start | bytes 1376264 | tf_op jit(solution)/shard_map/ppermute | solution.py:339
  58.1 12.7 %collective-permute-start.13 = (f32[14,64,128]{2,1,0:T(8,128)S(1)}, f32[14,64,128]{2,1,0:T(8,128)S(1)}, u32[]{:S(2)}, u32[]{:S(2)}) collective-permute-start(f32[14,64,128]{2,1,0:T(8,128)S(1)} %collective-permute-done.2.refs_4_), channel_id=1, source_target_pairs={{0,1},{1,0},{2,3},{3,2},{4,5},{5,4},{6,7},{7,6},{8,9},{9,8},{10,11... | collective-permute-start | bytes 1376264 | tf_op jit(solution)/shard_map/ppermute | solution.py:339
  58.1 13.1 %collective-permute-start.9 = (f32[14,64,128]{2,1,0:T(8,128)S(1)}, f32[14,64,128]{2,1,0:T(8,128)S(1)}, u32[]{:S(2)}, u32[]{:S(2)}) collective-permute-start(f32[14,64,128]{2,1,0:T(8,128)S(1)} %get-tuple-element.30.refs_0_), channel_id=1, source_target_pairs={{0,1},{1,0},{2,3},{3,2},{4,5},{5,4},{6,7},{7,6},{8,9},{9,8},{10,11... | collective-permute-start | bytes 1376264 | tf_op jit(solution)/shard_map/ppermute | solution.py:339
  58.6 12.7 %collective-permute-start.10 = (f32[14,64,128]{2,1,0:T(8,128)S(1)}, f32[14,64,128]{2,1,0:T(8,128)S(1)}, u32[]{:S(2)}, u32[]{:S(2)}) collective-permute-start(f32[14,64,128]{2,1,0:T(8,128)S(1)} %collective-permute-done.refs_2_.refs_1_), channel_id=1, source_target_pairs={{0,1},{1,0},{2,3},{3,2},{4,5},{5,4},{6,7},{7,6},{8,9},{9,8},{10,11... | collective-permute-start | bytes 1376264 | tf_op jit(solution)/shard_map/ppermute | solution.py:339
  70.3 3.4 %collective-permute-start.12 = (f32[14,64,128]{2,1,0:T(8,128)S(1)}, f32[14,64,128]{2,1,0:T(8,128)}, u32[]{:S(2)}, u32[]{:S(2)}) collective-permute-start(f32[14,64,128]{2,1,0:T(8,128)S(1)} %collective-permute-done.1.refs_3_), channel_id=1, source_target_pairs={{0,1},{1,0},{2,3},{3,2},{4,5},{5,4},{6,7},{7,6},{8,9},{9,8},{10,11... | collective-permute-start | bytes 1376264 | tf_op jit(solution)/shard_map/ppermute | solution.py:339
  70.6 3.0 %collective-permute-start.11 = (f32[14,64,128]{2,1,0:T(8,128)S(1)}, f32[14,64,128]{2,1,0:T(8,128)}, u32[]{:S(2)}, u32[]{:S(2)}) collective-permute-start(f32[14,64,128]{2,1,0:T(8,128)S(1)} %collective-permute-done.3.refs_1_.refs_2_), channel_id=1, source_target_pairs={{0,1},{1,0},{2,3},{3,2},{4,5},{5,4},{6,7},{7,6},{8,9},{9,8},{10,11... | collective-permute-start | bytes 1376264 | tf_op jit(solution)/shard_map/ppermute | solution.py:339
  70.8 2.8 %collective-permute-start.14 = (f32[14,64,128]{2,1,0:T(8,128)S(1)}, f32[14,64,128]{2,1,0:T(8,128)S(1)}, u32[]{:S(2)}, u32[]{:S(2)}) collective-permute-start(f32[14,64,128]{2,1,0:T(8,128)S(1)} %collective-permute-done.6.refs_5_), channel_id=1, source_target_pairs={{0,1},{1,0},{2,3},{3,2},{4,5},{5,4},{6,7},{7,6},{8,9},{9,8},{10,11... | collective-permute-start | bytes 1376264 | tf_op jit(solution)/shard_map/ppermute | solution.py:339
  71.2 3.1 %collective-permute-start.15 = (f32[14,64,128]{2,1,0:T(8,128)}, f32[14,64,128]{2,1,0:T(8,128)S(1)}, u32[]{:S(2)}, u32[]{:S(2)}) collective-permute-start(f32[14,64,128]{2,1,0:T(8,128)} %collective-permute-done.7.refs_6_), channel_id=1, source_target_pairs={{0,1},{1,0},{2,3},{3,2},{4,5},{5,4},{6,7},{7,6},{8,9},{9,8},{10,11... | collective-permute-start | bytes 1376264 | tf_op jit(solution)/shard_map/ppermute | solution.py:339
  72.7 2.1 %collective-permute-start.16 = (f32[14,64,128]{2,1,0:T(8,128)S(1)}, f32[14,64,128]{2,1,0:T(8,128)}, u32[]{:S(2)}, u32[]{:S(2)}) collective-permute-start(f32[14,64,128]{2,1,0:T(8,128)S(1)} %collective-permute-done.8.refs_7_), channel_id=1, source_target_pairs={{0,1},{1,0},{2,3},{3,2},{4,5},{5,4},{6,7},{7,6},{8,9},{9,8},{10,11... | collective-permute-start | bytes 1376264 | tf_op jit(solution)/shard_map/ppermute | solution.py:339
  (18 other events, 69.4 us)
